TPU v7x, 512 devices: a whole 4x4x16 slice. The times are simulated.
512 devices in a mesh: row: 16 (over z_hi, x, core), col: 32 (over y, z_lo).
Axes of the slice: x: 4, y: 4, z: 16 (z_hi: 2, z_lo: 8; z = z_hi * 8 + z_lo), core: 2. Of those that a mesh axis runs over, the one named last changes fastest.
Arguments:
- features: bfloat16 [65536, 256], P(('row', 'col')), may hold values from -6 to 6
- order: int32 [512, 128], P(('row', 'col')), may hold values from 0 to 127, each once within a row
- weight: bfloat16 [256, 256], replicated, may hold values from -0.375 to 0.375
- tile_values: bfloat16 [16, 32, 96, 128, 128], P('row', 'col'), may hold values from -0.375 to 0.375
- tile_list: int32 [16, 32, 96, 2], P('row', 'col'), may hold values from -1 to 31, as said below
- cotangent: bfloat16 [65536, 256], P(('row', 'col')), may hold values from -6 to 6
Outputs:
- activated: bfloat16 [65536, 256], P(('row', 'col'))
- feature_grad: bfloat16 [65536, 256], P(('row', 'col'))
- weight_grad: float32 [256, 256], replicated
Inputs may be any that keep to these rules, and one draw needn't show every extreme that they name: `tile_list`: on each grid cell the first k slots hold distinct pairs (block row below 32, block column below 16) and the other slots hold -1 in both entries; k is 2 or more everywhere and equals 96 on at least one cell.
All inputs are finite; a program needn't handle non-finite values.
Results may differ from a plain program's by a relative error of at most 0.027.
Values may be sent and summed in bfloat16 or wider, within the bound.
A program may use at most 64 MiB of HBM per device.

v0:
```python
import jax
import jax.numpy as jnp
from jax import lax
from jax.sharding import PartitionSpec as P


def block_products(adjacency_tiles, tile_pairs, source, out_blocks, transpose):
    tile_size = adjacency_tiles.shape[1]
    feature_width = source.shape[1]
    per_round = adjacency_tiles.shape[0] // 6
    occupied = jnp.sum((tile_pairs[:, 0] >= 0).astype(jnp.int32))
    rounds = (occupied + per_round - 1) // per_round
    source_blocks = source.reshape(-1, tile_size, feature_width)

    def advance(turn_index, accumulated):
        offset = (turn_index * per_round).astype(jnp.int32)
        tile_piece = lax.dynamic_slice_in_dim(adjacency_tiles, offset, per_round, 0)
        piece_pairs = lax.dynamic_slice_in_dim(tile_pairs, offset, per_round, 0)
        usable = piece_pairs[:, 0] >= 0
        if transpose:
            source_block = jnp.where(usable, piece_pairs[:, 0], 0)
            target_block = jnp.where(usable, piece_pairs[:, 1], out_blocks)
        else:
            source_block = jnp.where(usable, piece_pairs[:, 1], 0)
            target_block = jnp.where(usable, piece_pairs[:, 0], out_blocks)
        picked = jnp.take(source_blocks, source_block, axis=0)
        if transpose:
            products = jnp.einsum(
                "tij,tif->tjf", tile_piece, picked, preferred_element_type=jnp.float32
            )
        else:
            products = jnp.einsum(
                "tij,tjf->tif", tile_piece, picked, preferred_element_type=jnp.float32
            )
        return accumulated.at[target_block].add(products, mode="drop")

    accumulated = lax.fori_loop(
        0, rounds, advance, jnp.zeros((out_blocks, tile_size, feature_width), jnp.float32)
    )
    return accumulated.reshape(out_blocks * tile_size, feature_width)


def activation_grad(summed, cotangent):
    logistic = jax.nn.sigmoid(summed)
    return (cotangent.astype(jnp.float32) * logistic * (1.0 + summed * (1.0 - logistic))).astype(
        jnp.bfloat16
    )


def body(features, order, weight, tile_values, tile_list, cotangent):
    slab_rows = features.shape[0]
    positions = jnp.arange(slab_rows, dtype=jnp.int32)
    onehot = (order[0][:, None] == positions[None, :]).astype(jnp.bfloat16)
    clustered = jnp.dot(onehot, features, preferred_element_type=jnp.float32).astype(jnp.bfloat16)
    projected = jnp.dot(clustered, weight, preferred_element_type=jnp.float32).astype(jnp.bfloat16)
    columns = lax.all_gather(projected, "row", axis=0, tiled=True)
    adjacency_tiles = tile_values[0, 0]
    tile_pairs = tile_list[0, 0]
    tile_size = adjacency_tiles.shape[1]
    block_rows = lax.axis_size("col") * slab_rows // tile_size
    block_cols = lax.axis_size("row") * slab_rows // tile_size
    partial_value = block_products(adjacency_tiles, tile_pairs, columns, block_rows, False)
    summed = lax.psum_scatter(
        partial_value.astype(jnp.bfloat16), "col", scatter_dimension=0, tiled=True
    ).astype(jnp.float32)
    activated = jax.nn.silu(summed).astype(jnp.bfloat16)
    summed_grad = activation_grad(summed, cotangent)
    grad_rows = lax.all_gather(summed_grad, "col", axis=0, tiled=True)
    backward_partial = block_products(adjacency_tiles, tile_pairs, grad_rows, block_cols, True)
    backward = lax.psum_scatter(
        backward_partial.astype(jnp.bfloat16), "row", scatter_dimension=0, tiled=True
    ).astype(jnp.float32)
    local_grad = jnp.dot(
        clustered.astype(jnp.float32).T,
        backward,
        precision=lax.Precision.HIGHEST,
        preferred_element_type=jnp.float32,
    )
    weight_grad = lax.psum(local_grad, ("row", "col"))
    clustered_grad = jnp.dot(
        backward,
        weight.astype(jnp.float32).T,
        precision=lax.Precision.HIGHEST,
        preferred_element_type=jnp.float32,
    )
    feature_grad = jnp.dot(
        onehot.astype(jnp.float32).T,
        clustered_grad,
        precision=lax.Precision.HIGHEST,
        preferred_element_type=jnp.float32,
    )
    return (activated, feature_grad.astype(jnp.bfloat16), weight_grad)


def solution(mesh):
    placed = (
        P(("row", "col"), None),
        P(("row", "col"), None),
        P(),
        P("row", "col", None, None, None),
        P("row", "col", None, None),
        P(("row", "col"), None),
    )
    return jax.shard_map(
        body,
        mesh=mesh,
        in_specs=placed,
        out_specs=(P(("row", "col"), None), P(("row", "col"), None), P()),
        check_vma=False,
    )
```

profile of v0, /device:TPU:1, one launch (start us, length us, event | category | flops | bytes accessed | tf_op | source)
XLA Modules:
  0.0 1215.9 jit_solution(17676210650506795605)
XLA Ops:
  11.2 84.2 %all-gather.3.cloned.1.call-done = bf16[2048,256]{1,0:T(8,128)(2,1)} async-done(((bf16[128,256]{1,0:T(8,128)(2,1)}), bf16[2048,256]{1,0:T(8,128)(2,1)}) %all-gather.3.cloned.1.call-update) | async-done | bytes 1048592 | tf_op jit(solution)/shard_map/all_gather | solution.py:56
  95.4 2.4 broadcast_in_dim.38
  97.8 48.2 %while.20 = (s32[]{:T(128)}, f32[32,128,256]{2,1,0:T(8,128)}, s32[]{:T(128)}, s32[96,2]{0,1:T(2,128)S(1)}, bf16[96,128,128]{2,1,0:T(8,128)(2,1)}, /*index=5*/bf1...) while((s32[]{:T(128)}, f32[32,128,256]{2,1,0:T(8,128)}, s32[]{:T(128)}, ...), condition=%wide.region_3.4_spmd, body=%wide.region_1.3_spmd.sunk | while | flops 135267536 | bytes 12063683 | solution.py:37
  101.4 4.5 scatter_fusion
  109.4 4.5 scatter_fusion
  117.4 4.5 scatter_fusion
  125.4 4.5 scatter_fusion
  133.5 4.5 scatter_fusion
  141.5 4.5 scatter_fusion
  146.0 4.0 convert_element_type.46
  150.1 209.9 %reduce-scatter.3.cloned.1.call-done = bf16[128,256]{1,0:T(8,128)(2,1)} async-done(((bf16[4096,256]{1,0:T(8,128)(2,1)}), bf16[128,256]{1,0:T(8,128)(2,1)}) %reduce-scatter.3.cloned.1.call-update) | async-done | bytes 65552 | tf_op jit(solution)/shard_map/reduce_scatter | solution.py:63
  361.6 2.8 copy.9
  364.4 222.5 %all-gather.5.cloned.1.call-done = bf16[4096,256]{1,0:T(8,128)(2,1)} async-done(((bf16[128,256]{1,0:T(8,128)(2,1)}), bf16[4096,256]{1,0:T(8,128)(2,1)}) %all-gather.5.cloned.1.call-update) | async-done | bytes 2097168 | tf_op jit(solution)/shard_map/all_gather | solution.py:68
  588.4 49.8 %while.21 = (s32[]{:T(128)}, f32[16,128,256]{2,1,0:T(8,128)}, s32[]{:T(128)}, s32[96,2]{0,1:T(2,128)S(1)}, bf16[96,128,128]{1,2,0:T(8,128)(2,1)}, /*index=5*/bf1...) while((s32[]{:T(128)}, f32[16,128,256]{2,1,0:T(8,128)}, s32[]{:T(128)}, ...), condition=%wide.region_7.8_spmd, body=%wide.region_5.7_spmd.sunk | while | flops 135267536 | bytes 12063683 | solution.py:37
  588.5 2.2 gather_fusion.1
  592.3 4.4 scatter_fusion.1
  600.6 4.4 scatter_fusion.1
  608.9 4.4 scatter_fusion.1
  617.2 4.4 scatter_fusion.1
  625.5 4.5 scatter_fusion.1
  633.9 4.4 scatter_fusion.1
  638.2 2.7 convert_element_type.52
  641.0 112.8 %reduce-scatter.5.cloned.1.call-done = bf16[128,256]{1,0:T(8,128)(2,1)} async-done(((bf16[2048,256]{1,0:T(8,128)(2,1)}), bf16[128,256]{1,0:T(8,128)(2,1)}) %reduce-scatter.5.cloned.1.call-update) | async-done | bytes 65552 | tf_op jit(solution)/shard_map/reduce_scatter | solution.py:70
  757.6 450.2 %all-reduce.2.cloned.1.call-done = f32[256,256]{1,0:T(8,128)} async-done(((f32[256,256]{1,0:T(8,128)}), f32[256,256]{1,0:T(8,128)}) %all-reduce.2.cloned.1.call-update) | async-done | bytes 262160 | tf_op jit(solution)/shard_map/psum | solution.py:79
  (100 shorter events, 53.9 us)
Async XLA Ops:
  7.2 1.2 copy-start
  7.2 88.2 %all-gather.3.cloned.1.call-start = ((), (), s32[]{:S(2)}) async-start(), calls=%async_computation.2 | async-start | bytes 1114112 | tf_op jit(solution)/shard_map/all_gather | solution.py:56
  9.1 350.8 %reduce-scatter.3.cloned.1.call-start = ((), (), s32[]{:S(2)}) async-start(), calls=%async_computation.3 | async-start | bytes 2162688 | tf_op jit(solution)/shard_map/reduce_scatter | solution.py:63
  95.4 2.4 copy-start.2
  146.0 215.5 %copy-start.1 = (bf16[96,128,128]{2,1,0:T(8,128)(2,1)S(1)}, bf16[96,128,128]{2,1,0:T(8,128)(2,1)}, u32[]{:S(2)}) copy-start(bf16[96,128,128]{2,1,0:T(8,128)(2,1)} %get-tuple-element.259) | copy-start | bytes 9437188
  150.0 209.9 %copy-start.3 = (bf16[128,256]{1,0:T(8,128)(2,1)S(1)}, bf16[128,256]{1,0:T(8,128)(2,1)}, u32[]{:S(2)}) copy-start(bf16[128,256]{1,0:T(8,128)(2,1)} %param.15) | copy-start | bytes 196612
  150.0 436.8 %all-gather.5.cloned.1.call-start = ((), (), s32[]{:S(2)}) async-start(), calls=%async_computation.4 | async-start | bytes 2162688 | tf_op jit(solution)/shard_map/all_gather | solution.py:68
  361.5 392.3 %reduce-scatter.5.cloned.1.call-start = ((), (), s32[]{:S(2)}) async-start(), calls=%async_computation.5 | async-start | bytes 1114112 | tf_op jit(solution)/shard_map/reduce_scatter | solution.py:70
  638.2 118.4 %copy-start.4 = (s32[1,128]{1,0:T(1,128)S(1)}, s32[1,128]{1,0:T(1,128)}, u32[]{:S(2)}) copy-start(s32[1,128]{1,0:T(1,128)} %param.11) | copy-start | bytes 1540
  641.0 566.7 %all-reduce.2.cloned.1.call-start = ((), (), s32[]{:S(2)}) async-start(), calls=%async_computation.6 | async-start | bytes 524288 | tf_op jit(solution)/shard_map/psum | solution.py:79
Sparse Core Ops, SparseCore 0:
  11.9 83.4 all-gather.2
  150.1 209.7 reduce-scatter.2
  362.8 223.9 all-gather.4
  641.1 112.6 reduce-scatter.4
  759.6 448.0 all-reduce.1
where the time goes:
time: 1220 us
  waiting for transfers between devices  1080 us (89%)
  other arithmetic  63.5 us (5%)
  local copies, waits for them, and re-layouts  33.6 us (3%)
  matrix products  24.3 us (2%)
  between operations  14.5 us (1%)
    psum x1, waiting for transfers between devices, body(): weight_grad = lax.psum(local_grad, ('row', 'col'))  450 us
    all_gather x1, waiting for transfers between devices, body(): grad_rows = lax.all_gather(summed_grad, 'col', axis=0, tiled=True)  222 us
    reduce_scatter x1, waiting for transfers between devices, body(): lax.psum_scatter(partial_value.astype(jnp.bfloat16), 'col', scatter_dimen...  210 us
    reduce_scatter x1, waiting for transfers between devices, body(): lax.psum_scatter(backward_partial.astype(jnp.bfloat16), 'row', scatter_di...  113 us
    all_gather x1, waiting for transfers between devices, body(): columns = lax.all_gather(projected, 'row', axis=0, tiled=True)  84.2 us
    scatter-add x12, other arithmetic, advance(): return accumulated.at[target_block].add(products, mode='drop')  53.7 us
  transfers between devices with their start and end apart: 5, of which 5 were waited for; matrix products, arithmetic and copies ran while one was open for 1% of the time, Pallas kernels for 0%

commit v1 on v0

v1 whole, which is shorter than its diff:
```python
import jax
import jax.numpy as jnp
from jax import lax
from jax.experimental import pallas as pl
from jax.experimental.pallas import tpu as pltpu
from jax.sharding import PartitionSpec as P

MESH = pl.DeviceIdType.MESH
F32 = jnp.float32
BF16 = jnp.bfloat16
VMEM_LIMIT = 48 << 20


def position():
    row, col = lax.axis_index("row"), lax.axis_index("col")
    return row // 8, row // 2 % 4, row % 2, col // 8, col % 8


def device(zh, x, k, y, zl):
    return {"row": zh * 8 + x * 2 + k, "col": y * 8 + zl}


def remote(src, dst, send, recv, target):
    return pltpu.make_async_remote_copy(
        src_ref=src, dst_ref=dst, send_sem=send, recv_sem=recv, device_id=target, device_id_type=MESH
    )


def meet(targets):
    barrier = pltpu.get_barrier_semaphore()
    for target in targets:
        pl.semaphore_signal(barrier, inc=1, device_id=target, device_id_type=MESH)
    pl.semaphore_wait(barrier, len(targets))


def dot(a, b, dims):
    return lax.dot_general(a, b, (dims, ((), ())), preferred_element_type=F32)


def split_dot(a, b, dims):
    high = a.astype(BF16)
    low = (a - high.astype(F32)).astype(BF16)
    return dot(high, b, dims) + dot(low, b, dims)


def chosen(order_ref):
    rows = lax.broadcasted_iota(jnp.int32, (128, 128), 0)
    return jnp.where(rows == order_ref[...], 1.0, 0.0).astype(BF16)


def gather_row_kernel(features, order, blocks, send, recv):
    zh, x, k, y, zl = position()
    sibling = device(zh, x, 1 - k, y, zl)
    other = device(1 - zh, x, k, y, zl)
    beside = [device(zh, (x + d) % 4, k, y, zl) for d in (1, 3, 2)]
    mine = zh * 8 + x * 2 + k
    far = (1 - zh) * 8 + x * 2 + k
    blocks[mine] = dot(chosen(order), features[...], ((0,), (0,))).astype(BF16)
    meet([sibling, other] + beside)
    copies = []

    def push(slot, target):
        copy = remote(blocks.at[slot], blocks.at[slot], send.at[len(copies)], recv.at[slot], target)
        copy.start()
        copies.append(copy)

    def arrived(slot):
        remote(blocks.at[slot], blocks.at[slot], send.at[0], recv.at[slot], sibling).wait_recv()

    push(mine, other)
    for target in beside:
        push(mine, target)
    push(mine, sibling)
    for d in (1, 3, 2):
        slot = zh * 8 + (x + d) % 4 * 2 + k
        arrived(slot)
        push(slot, sibling)
    arrived(far)
    for target in beside:
        push(far, target)
    push(far, sibling)
    for d in (1, 3, 2):
        slot = (1 - zh) * 8 + (x + d) % 4 * 2 + k
        arrived(slot)
        push(slot, sibling)
    for n in range(8):
        arrived(n * 2 + 1 - k)
    for copy in copies:
        copy.wait_send()


def gather_row(features, order):
    return pl.pallas_call(
        gather_row_kernel,
        out_shape=jax.ShapeDtypeStruct((16, 128, 256), BF16),
        in_specs=[pl.BlockSpec(memory_space=pltpu.VMEM)] * 2,
        out_specs=pl.BlockSpec(memory_space=pltpu.VMEM),
        scratch_shapes=[pltpu.SemaphoreType.DMA((16,)), pltpu.SemaphoreType.DMA((16,))],
        compiler_params=pltpu.CompilerParams(collective_id=0, has_side_effects=True, vmem_limit_bytes=VMEM_LIMIT),
        name="gather_row",
    )(features, order)


def products_kernel(transpose, out_blocks, pairs, tiles, source, out, total):
    total[...] = jnp.zeros_like(total)
    unroll = 4

    def step(i, carry):
        picked = []
        for j in range(unroll):
            t = i * unroll + j
            p, q = pairs[2 * t], pairs[2 * t + 1]
            usable = p >= 0
            src, dst = (p, q) if transpose else (q, p)
            src = jnp.where(usable, src, 0)
            dst = jnp.where(usable, dst, out_blocks)
            dims = ((0,), (0,)) if transpose else ((1,), (0,))
            picked.append((dst, dot(tiles[t], source[src], dims)))
        for dst, product in picked:
            total[dst] += product
        return carry

    lax.fori_loop(0, tiles.shape[0] // unroll, step, 0)

    def finish(b, carry):
        out[b] = total[b].astype(BF16)
        return carry

    lax.fori_loop(0, out_blocks, finish, 0)


def products(pairs, tiles, source, out_blocks, transpose):
    def kernel(*refs):
        products_kernel(transpose, out_blocks, *refs)

    return pl.pallas_call(
        kernel,
        out_shape=jax.ShapeDtypeStruct((out_blocks, 128, 256), BF16),
        in_specs=[pl.BlockSpec(memory_space=pltpu.SMEM)] + [pl.BlockSpec(memory_space=pltpu.VMEM)] * 2,
        out_specs=pl.BlockSpec(memory_space=pltpu.VMEM),
        scratch_shapes=[pltpu.VMEM((out_blocks + 1, 128, 256), F32)],
        compiler_params=pltpu.CompilerParams(vmem_limit_bytes=VMEM_LIMIT),
        name="products_back" if transpose else "products",
    )(pairs, tiles, source)


def middle_kernel(
    part, weight, cotangent, activated, grad, piece,
    from_a, from_d, from_s, staged, summed_y, from_z,
    wg, wg_core, wg_y, wg_z, wg_row, wg_sent,
    send_a, send_d, send_s, send_z, recv_a, recv_d, recv_s, recv_z,
    gather_send, gather_recv, wg_send, wg_recv,
):
    zh, x, k, y, zl = position()

    def on_y(d):
        return device(zh, x, k, (y + d + 4) % 4, zl)

    def on_z(z):
        return device(zh, x, k, y, z)

    def block(yy, c):
        return (yy + 4) % 4 * 8 + c

    sibling = device(zh, x, 1 - k, y, zl)
    z_peers = [on_z((zl + d) % 8) for d in range(1, 8)]
    y_peers = [on_y(d) for d in range(1, 4)]
    row_peers = [device((zh + d // 4) % 2, (x + d) % 4, k, y, zl) for d in range(1, 8)]
    meet([sibling] + z_peers + y_peers + row_peers)

    edge = zl + zl // 4 * (7 - 2 * zl)
    inward = 1 - 2 * (zl // 4)

    def ranked(m):
        both = (2 * edge - m + 8) // 8
        alternate = 1 if m % 2 else -1
        way = both * alternate + (1 - both) * inward
        return zl + both * alternate * ((m + 1) // 2) + (1 - both) * inward * (m - edge), way

    order = [ranked(m) for m in range(7, 0, -1)] + [(zl, 0)]
    chunk = [c for c, _ in order]
    turn = [1 - 2 * (c % 2) for c in chunk]
    copies = []

    def go(copy):
        copy.start()
        copies.append(copy)

    def send_antipode(i):
        c = chunk[i]
        go(remote(part.at[block(y + 2, c)], from_a.at[c], send_a.at[c], recv_a.at[c], on_y(turn[i])))

    def send_direct(i):
        c = chunk[i]
        go(remote(part.at[block(y - turn[i], c)], from_d.at[c], send_d.at[c], recv_d.at[c], on_y(-turn[i])))

    def landed(buffer, sem):
        remote(buffer, buffer, sem, sem, sibling).wait_recv()

    def send_sum(i):
        c = chunk[i]
        landed(from_a.at[c], recv_a.at[c])
        staged[c] = (part[block(y + turn[i], c)].astype(F32) + from_a[c].astype(F32)).astype(BF16)
        go(remote(staged.at[c], from_s.at[c], send_s.at[c], recv_s.at[c], on_y(turn[i])))

    def sum_y(i):
        c = chunk[i]
        landed(from_d.at[c], recv_d.at[c])
        landed(from_s.at[c], recv_s.at[c])
        return part[block(y, c)].astype(F32) + from_d[c].astype(F32) + from_s[c].astype(F32)

    def along_z(i):
        c, way = order[i]
        total = sum_y(i)

        @pl.when(edge > 0)
        def _():
            landed(from_z.at[c], recv_z.at[c])
            summed_y[c] = (total + from_z[c].astype(F32)).astype(BF16)

        @pl.when(edge == 0)
        def _():
            summed_y[c] = total.astype(BF16)

        near = (7 - way * (c - zl)) // 6
        slot = c + near * ((1 - way) // 2) * (8 - c)
        go(remote(summed_y.at[c], from_z.at[slot], send_z.at[c], recv_z.at[slot], on_z(zl + way)))

    send_antipode(0)
    send_antipode(1)
    send_direct(0)
    for i in range(8):
        if i + 2 < 8:
            send_antipode(i + 2)
        if i + 1 < 8:
            send_direct(i + 1)
        send_sum(i)
        if i >= 1:
            along_z(i - 1)
    own = sum_y(7)

    @pl.when(zl > 0)
    def _():
        landed(from_z.at[zl], recv_z.at[zl])

    @pl.when(zl < 7)
    def _():
        landed(from_z.at[8], recv_z.at[8])

    left = jnp.where(zl > 0, from_z[zl].astype(F32), 0.0)
    right = jnp.where(zl < 7, from_z[8].astype(F32), 0.0)
    own = own + left + right

    summed = split_dot(own, weight[...], ((1,), (0,)))
    logistic = 1.0 / (1.0 + jnp.exp(-summed))
    gradient = (cotangent[...].astype(F32) * logistic * (1.0 + summed * (1.0 - logistic))).astype(BF16)
    mine = block(y, zl)
    grad[mine] = gradient

    def arrived(slot):
        landed(grad.at[slot], gather_recv.at[slot])

    def pass_on(slot, lane, m, target):
        go(remote(grad.at[slot], grad.at[slot], gather_send.at[lane, m], gather_recv.at[slot], target))

    def conditional(slot, lane, target):
        return remote(grad.at[slot], grad.at[slot], gather_send.at[lane, 0], gather_recv.at[slot], target)

    up = conditional(mine, 0, on_z((zl + 1) % 8))
    down = conditional(mine, 3, on_z((zl + 7) % 8))

    @pl.when(zl < 7)
    def _():
        up.start()

    @pl.when(zl > 0)
    def _():
        down.start()

    pass_on(mine, 1, 0, on_y(1))
    pass_on(mine, 2, 0, on_y(-1))
    activated[...] = (summed * logistic).astype(BF16)
    wg[...] = split_dot_left(own, gradient)
    core_copy = remote(wg.at[pl.ds((1 - k) * 128, 128)], wg_core, wg_send.at[0], wg_recv.at[0], sibling)
    go(core_copy)

    def wg_after_core():
        core_copy.wait_recv()
        wg[pl.ds(pl.multiple_of(k * 128, 128), 128)] += wg_core[...]
        for d in (1, 2, 3):
            rows = pl.ds(pl.multiple_of(k * 128 + (y + d) % 4 * 32, 32), 32)
            go(remote(wg.at[rows], wg_y.at[d], wg_send.at[d], wg_recv.at[d], y_peers[d - 1]))

    def wg_after_y():
        rows = pl.ds(pl.multiple_of(k * 128 + y * 32, 32), 32)
        total = wg[rows]
        for d in (1, 2, 3):
            landed(wg_y.at[d], wg_recv.at[d])
            total = total + wg_y[d]
        for j in range(8):
            wg_sent[j] = total[8 * (j // 2): 8 * (j // 2) + 8, 128 * (j % 2): 128 * (j % 2) + 128]
        for d in range(1, 8):
            go(remote(wg_sent.at[(zl + d) % 8], wg_z.at[d], wg_send.at[3 + d], wg_recv.at[3 + d], z_peers[d - 1]))

    def wg_after_z():
        total = wg_sent[zl]
        for d in range(1, 8):
            landed(wg_z.at[d], wg_recv.at[3 + d])
            total = total + wg_z[d]
        here = zh * 4 + x
        wg_row[here] = total
        for d in range(1, 8):
            go(remote(wg_row.at[here], wg_row.at[here], wg_send.at[10 + d], wg_recv.at[11 + here], row_peers[d - 1]))

    def wg_after_row():
        for d in range(1, 8):
            slot = (zh + d // 4) % 2 * 4 + (x + d) % 4
            landed(wg_row.at[slot], wg_recv.at[11 + slot])
        total = wg_row[0]
        for n in range(1, 8):
            total = total + wg_row[n]
        piece[...] = total

    spread = [(zl, 0)] + [ranked(m) for m in range(1, 8)]
    z_copies = []

    def across(m):
        c = spread[m][0]
        e = 1 - 2 * (c % 2)
        slot = block(y - e, c)
        arrived(slot)
        pass_on(slot, 3 if m else 4, m, on_y(e))

    for m in range(1, 8):
        c, way = spread[m]
        slot = block(y, c)
        arrived(slot)
        forward = remote(
            grad.at[slot], grad.at[slot], gather_send.at[0, m], gather_recv.at[slot], on_z((zl - way + 8) % 8)
        )
        z_copies.append(forward)

        @pl.when(edge > 0)
        def _():
            forward.start()

        pass_on(slot, 1, m, on_y(1))
        pass_on(slot, 2, m, on_y(-1))
        across(m - 1)
        if m == 2:
            wg_after_core()
        if m == 4:
            wg_after_y()
        if m == 6:
            wg_after_z()
    across(7)
    wg_after_row()
    for c in range(8):
        e = 1 - 2 * (c % 2)
        arrived(block(y + e, c))
        arrived(block(y + 2, c))

    @pl.when(zl < 7)
    def _():
        up.wait_send()

    @pl.when(zl > 0)
    def _():
        down.wait_send()

    @pl.when(edge > 0)
    def _():
        for forward in z_copies:
            forward.wait_send()

    for copy in copies:
        copy.wait_send()


def split_dot_left(a, b):
    return split_dot(a, b, ((0,), (0,)))


def middle(part, weight, cotangent):
    slabs = lambda n: pltpu.VMEM((n, 128, 256), BF16)
    dma = pltpu.SemaphoreType.DMA
    return pl.pallas_call(
        middle_kernel,
        out_shape=(
            jax.ShapeDtypeStruct((128, 256), BF16),
            jax.ShapeDtypeStruct((32, 128, 256), BF16),
            jax.ShapeDtypeStruct((8, 128), F32),
        ),
        in_specs=[pl.BlockSpec(memory_space=pltpu.VMEM)] * 3,
        out_specs=(pl.BlockSpec(memory_space=pltpu.VMEM),) * 3,
        scratch_shapes=[
            slabs(8), slabs(8), slabs(8), slabs(8), slabs(8), slabs(9),
            pltpu.VMEM((256, 256), F32), pltpu.VMEM((128, 256), F32), pltpu.VMEM((4, 32, 256), F32),
            pltpu.VMEM((8, 8, 128), F32), pltpu.VMEM((8, 8, 128), F32), pltpu.VMEM((8, 8, 128), F32),
            dma((8,)), dma((8,)), dma((8,)), dma((8,)), dma((8,)), dma((8,)), dma((8,)), dma((9,)),
            dma((5, 8)), dma((32,)), dma((18,)), dma((19,)),
        ],
        compiler_params=pltpu.CompilerParams(collective_id=1, has_side_effects=True, vmem_limit_bytes=VMEM_LIMIT),
        name="middle",
    )(part, weight, cotangent)


def tail_kernel(
    part, weight, order, piece, feature_grad, weight_grad,
    from_core, staged, from_x, own, z_out, from_z, pieces,
    send_core, recv_core, send_x, recv_x, send_z, recv_z, wg_send, wg_z_recv, wg_y_recv, wg_core_recv,
):
    zh, x, k, y, zl = position()
    sibling = device(zh, x, 1 - k, y, zl)
    other = device(1 - zh, x, k, y, zl)
    beside = [device(zh, (x + d) % 4, k, y, zl) for d in range(1, 4)]
    z_peers = [device(zh, x, k, y, (zl + d) % 8) for d in range(1, 8)]
    y_peers = [device(zh, x, k, (y + d) % 4, zl) for d in range(1, 4)]
    pieces[k, y, zl] = piece[...]
    meet([sibling, other] + beside + z_peers + y_peers)
    copies = []

    def go(copy):
        copy.start()
        copies.append(copy)

    def landed(buffer, sem):
        remote(buffer, buffer, sem, sem, sibling).wait_recv()

    turns = [((zh + h) % 2, d) for h in (1, 0) for d in (2, 1, 3, 0)]
    for h, d in turns:
        slot = h * 4 + (x + d) % 4
        go(remote(part.at[slot * 2 + 1 - k], from_core.at[slot], send_core.at[slot], recv_core.at[slot], sibling))
    for d in range(1, 8):
        here = pieces.at[k, y, zl]
        go(remote(here, here, wg_send.at[d], wg_z_recv.at[zl], z_peers[d - 1]))
    for h, d in turns[:4] + turns[4:]:
        slot = h * 4 + (x + d) % 4
        landed(from_core.at[slot], recv_core.at[slot])
        total = part[slot * 2 + k].astype(F32) + from_core[slot].astype(F32)
        if d:
            staged[slot] = total.astype(BF16)
            go(remote(
                staged.at[slot], from_x.at[h * 4 + d], send_x.at[slot], recv_x.at[h * 4 + d], beside[d - 1]
            ))
        else:
            own[h] = total

    for d in range(1, 8):
        landed(pieces.at[k, y, (zl + d) % 8], wg_z_recv.at[(zl + d) % 8])
    for d in range(1, 4):
        here = pieces.at[k, y]
        go(remote(here, here, wg_send.at[7 + d], wg_y_recv.at[y], y_peers[d - 1]))

    def sum_x(h):
        total = own[h]
        for d in range(1, 4):
            landed(from_x.at[h * 4 + d], recv_x.at[h * 4 + d])
            total = total + from_x[h * 4 + d].astype(F32)
        return total

    z_out[...] = sum_x(1 - zh).astype(BF16)
    z_copy = remote(z_out, from_z, send_z, recv_z, other)
    go(z_copy)
    for d in range(1, 4):
        landed(pieces.at[k, (y + d) % 4], wg_y_recv.at[(y + d) % 4])
    core_copy = remote(pieces.at[k], pieces.at[k], wg_send.at[0], wg_core_recv, sibling)
    go(core_copy)
    backward = sum_x(zh)
    landed(pieces.at[1 - k], wg_core_recv)
    for kk in range(2):
        for yy in range(4):
            for j in range(8):
                row = kk * 128 + yy * 32 + j // 2 * 8
                weight_grad[row:row + 8, j % 2 * 128:j % 2 * 128 + 128] = pieces[kk, yy, j]
    z_copy.wait_recv()
    backward = backward + from_z[...].astype(F32)
    clustered_grad = split_dot(backward, weight[...], ((1,), (1,))).astype(BF16)
    feature_grad[...] = dot(chosen(order), clustered_grad, ((1,), (0,))).astype(BF16)
    for copy in copies:
        copy.wait_send()


def tail(part, weight, order, piece):
    dma = pltpu.SemaphoreType.DMA
    slabs = lambda n: pltpu.VMEM((n, 128, 256), BF16)
    return pl.pallas_call(
        tail_kernel,
        out_shape=(jax.ShapeDtypeStruct((128, 256), BF16), jax.ShapeDtypeStruct((256, 256), F32)),
        in_specs=[pl.BlockSpec(memory_space=pltpu.VMEM)] * 4,
        out_specs=(pl.BlockSpec(memory_space=pltpu.VMEM),) * 2,
        scratch_shapes=[
            slabs(8), slabs(8), slabs(8), pltpu.VMEM((2, 128, 256), F32),
            pltpu.VMEM((128, 256), BF16), pltpu.VMEM((128, 256), BF16), pltpu.VMEM((2, 4, 8, 8, 128), F32),
            dma((8,)), dma((8,)), dma((8,)), dma((8,)), dma, dma, dma((11,)), dma((8,)), dma((4,)), dma,
        ],
        compiler_params=pltpu.CompilerParams(collective_id=2, has_side_effects=True, vmem_limit_bytes=VMEM_LIMIT),
        name="tail",
    )(part, weight, order, piece)


def body(features, order, weight, tile_values, tile_list, cotangent):
    tiles = tile_values[0, 0]
    pairs = tile_list[0, 0].reshape(-1)
    columns = gather_row(features, order)
    part = products(pairs, tiles, columns, 32, False)
    activated, grad, piece = middle(part, weight, cotangent)
    back = products(pairs, tiles, grad, 16, True)
    feature_grad, weight_grad = tail(back, weight, order, piece)
    return activated, feature_grad, weight_grad


def solution(mesh):
    placed = (
        P(("row", "col"), None),
        P(("row", "col"), None),
        P(),
        P("row", "col", None, None, None),
        P("row", "col", None, None),
        P(("row", "col"), None),
    )
    return jax.shard_map(
        body,
        mesh=mesh,
        in_specs=placed,
        out_specs=(P(("row", "col"), None), P(("row", "col"), None), P()),
        check_vma=False,
    )
```

time: 1220 us -> 163 us (0.13)
  waiting for transfers between devices: 1080 us -> 0 us
  Pallas kernels: 0 us -> 158 us
  other arithmetic: 63.5 us -> 0 us
  local copies, waits for them, and re-layouts: 33.6 us -> 4.38 us
  matrix products: 24.3 us -> 0 us
  between operations: 14.5 us -> 0.73 us
    psum x1 -> x0, waiting for transfers between devices: 450 us -> none  [body(): weight_grad = lax.psum(local_grad, ('row', 'col'))]
    reduce_scatter x2 -> x0, waiting for transfers between devices: 323 us -> none  [the longest x1 210 us: body(): lax.psum_scatter(partial_value.astype(jnp.bfloat16), 'col', scatter_dimen...]
    all_gather x2 -> x0, waiting for transfers between devices: 307 us -> none  [the longest x1 222 us: body(): grad_rows = lax.all_gather(summed_grad, 'col', axis=0, tiled=True)]
    pallas_call x0 -> x5, Pallas kernels: none -> 158 us  [the longest x1 77.9 us: middle(): pl.pallas_call(middle_kernel, out_shape=(jax.ShapeDtypeStruct((128, 256),...]
    scatter-add x12 -> x0, other arithmetic: 53.7 us -> none  [advance(): return accumulated.at[target_block].add(products, mode='drop')]
    dot_general x17 -> x0, matrix products: 24.3 us -> none  [the longest x6 9.32 us: advance(): jnp.einsum('tij,tjf->tif', tile_piece, picked, preferred_element_type=jnp...]
    gather x12 -> x0, local copies, waits for them, and re-layouts: 24.3 us -> none  [advance(): picked = jnp.take(source_blocks, source_block, axis=0)]
  transfers between devices with their start and end apart: 5 -> 0, of which waited for: 5 -> 0; matrix products, arithmetic and copies ran while one was open for 1% -> 0% of each run, Pallas kernels for 0% -> 0%
where the time goes in v1:
time: 163 us
  Pallas kernels  158 us (97%)
  local copies, waits for them, and re-layouts  4.38 us (3%)
    pallas_call x1, Pallas kernels, middle(): pl.pallas_call(middle_kernel, out_shape=(jax.ShapeDtypeStruct((128, 256),...  77.9 us
    pallas_call x1, Pallas kernels, tail(): pl.pallas_call(tail_kernel, out_shape=(jax.ShapeDtypeStruct((128, 256), B...  35.8 us
    pallas_call x1, Pallas kernels, gather_row(): pl.pallas_call(gather_row_kernel, out_shape=jax.ShapeDtypeStruct((16, 128...  27.7 us
    pallas_call x2, Pallas kernels, products(): pl.pallas_call(kernel, out_shape=jax.ShapeDtypeStruct((out_blocks, 128, 2...  16.7 us
    unnamed x14, local copies, waits for them, and re-layouts  4.25 us

profile of v1, /device:TPU:1, one launch (start us, length us, event | category | flops | bytes accessed | tf_op | source)
XLA Modules:
  0.0 163.2 jit_solution(7069396100224475920)
XLA Ops:
  0.6 0.8 copy.9
  1.4 0.1 reshape_squeeze.3.refs_0_
  1.5 0.0 copy-start.1
  1.6 0.8 copy-done.1
  2.4 0.0 copy-start.3
  2.4 0.7 copy-done.3
  3.0 27.7 %gather_row.1.refs_2_ = bf16[16,128,256]{2,1,0:T(8,128)(2,1)S(1)} custom-call(bf16[128,256]{1,0:T(8,128)(2,1)S(1)} %copy-done.1, s32[1,128]{1,0:T(1,128)S(1)} %copy-done.3), custom_call_target="tpu_custom_call" | custom-call | tf_op jit(solution)/shard_map/gather_row/pallas_call | solution.py:93
  30.7 0.0 copy-start
  30.7 0.0 copy-start.2
  30.8 8.1 %products.1.part = bf16[32,128,256]{2,1,0:T(8,128)(2,1)S(1)} custom-call(s32[192]{0:T(256)S(1)} %reshape_squeeze.3.refs_0_, bf16[96,128,128]{2,1,0:T(8,128)(2,1)} %bitcast.3, bf16[16,128,256]{2,1,0:T(8,128)(2,1)S(1)} %gather_row.1.refs_2_), custom_call_target="tpu_custom_call" | custom-call | tf_op jit(solution)/shard_map/products/pallas_call | solution.py:136
  38.9 0.0 copy-done
  38.9 0.0 copy-done.2
  38.9 77.9 %middle.1 = (bf16[128,256]{1,0:T(8,128)(2,1)S(1)}, bf16[32,128,256]{2,1,0:T(8,128)(2,1)S(1)}, f32[8,128]{1,0:T(8,128)S(1)}) custom-call(bf16[32,128,256]{2,1,0:T(8,128)(2,1)S(1)} %products.1.part, bf16[256,256]{1,0:T(8,128)(2,1)S(1)} %copy-done, bf16[128,256]{1,0:T(8,128)(2,1)S(1)} %copy-done.2), custom_call_target="tpu_custom_call" | custom-call | tf_op jit(solution)/shard_map/middle/pallas_call | solution.py:387
  116.8 0.0 copy-start.4
  116.8 8.6 %products_back.1.part = bf16[16,128,256]{2,1,0:T(8,128)(2,1)S(1)} custom-call(s32[192]{0:T(256)S(1)} %reshape_squeeze.3.refs_0_, bf16[96,128,128]{2,1,0:T(8,128)(2,1)} %bitcast.4, bf16[32,128,256]{2,1,0:T(8,128)(2,1)S(1)} %get-tuple-element.9.refs_2_), custom_call_target="tpu_custom_call" | custom-call | tf_op jit(solution)/shard_map/products_back/pallas_call | solution.py:136
  125.4 0.0 copy-done.4
  125.4 35.8 %tail.1 = (bf16[128,256]{1,0:T(8,128)(2,1)S(1)}, f32[256,256]{1,0:T(8,128)S(1)}) custom-call(bf16[16,128,256]{2,1,0:T(8,128)(2,1)S(1)} %products_back.1.part, bf16[256,256]{1,0:T(8,128)(2,1)S(1)} %copy-done, s32[1,128]{1,0:T(1,128)S(1)} %copy-done.4, f32[8,128]{1,0:T(8,128)S(1)} %get-tuple-element.10.piece), custom_call_target="tpu_custom_call" | custom-call | tf_op jit(solution)/shard_map/tail/pallas_call | solution.py:487
  161.2 0.6 copy.13
  161.8 0.6 copy.14
  162.5 0.7 copy.15
Async XLA Ops:
  1.5 0.8 copy-start.1
  2.4 0.7 copy-start.3
  30.7 8.1 %copy-start = (bf16[256,256]{1,0:T(8,128)(2,1)S(1)}, bf16[256,256]{1,0:T(8,128)(2,1)}, u32[]{:S(2)}) copy-start(bf16[256,256]{1,0:T(8,128)(2,1)} %weight.3) | copy-start | bytes 393220
  30.7 8.1 %copy-start.2 = (bf16[128,256]{1,0:T(8,128)(2,1)S(1)}, bf16[128,256]{1,0:T(8,128)(2,1)}, u32[]{:S(2)}) copy-start(bf16[128,256]{1,0:T(8,128)(2,1)} %cotangent.1) | copy-start | bytes 196612
  116.8 8.6 %copy-start.4 = (s32[1,128]{1,0:T(1,128)S(1)}, s32[1,128]{1,0:T(1,128)}, u32[]{:S(2)}) copy-start(s32[1,128]{1,0:T(1,128)} %order.3) | copy-start | bytes 1540

commit v2 on v0

v2 whole, which is shorter than its diff:
```python
import jax
import jax.numpy as jnp
from jax import lax
from jax.experimental import pallas as pl
from jax.experimental.pallas import tpu as pltpu
from jax.sharding import PartitionSpec as P

MESH = pl.DeviceIdType.MESH
F32 = jnp.float32
BF16 = jnp.bfloat16
VMEM_LIMIT = 56 << 20


def position():
    row, col = lax.axis_index("row"), lax.axis_index("col")
    return row // 8, row // 2 % 4, row % 2, col // 8, col % 8


def device(zh, x, k, y, zl):
    return {"row": zh * 8 + x * 2 + k, "col": y * 8 + zl}


def remote(src, dst, send, recv, target):
    return pltpu.make_async_remote_copy(
        src_ref=src, dst_ref=dst, send_sem=send, recv_sem=recv, device_id=target, device_id_type=MESH
    )


def dot(a, b, dims):
    return lax.dot_general(a, b, (dims, ((), ())), preferred_element_type=F32)


def split_dot(a, b, dims):
    high = a.astype(BF16)
    low = (a - high.astype(F32)).astype(BF16)
    return dot(high, b, dims) + dot(low, b, dims)


def chosen(order):
    rows = lax.broadcasted_iota(jnp.int32, (128, 128), 0)
    return jnp.where(rows == order, 1.0, 0.0).astype(BF16)


def tables(pairs, table):
    n = pairs.shape[1]
    down = lax.broadcasted_iota(jnp.int32, (n, n), 0)
    across = lax.broadcasted_iota(jnp.int32, (n, n), 1)
    same = down == across

    def column(row):
        return jnp.sum(jnp.where(same, row, 0), axis=1, keepdims=True)

    p_row, q_row = pairs[0:1, :], pairs[1:2, :]
    lane = lax.broadcasted_iota(jnp.int32, (1, n), 1)
    for base, major_row, minor_row in ((0, p_row, q_row), (4, q_row, p_row)):
        key_row = jnp.where(p_row >= 0, major_row * 32 + minor_row, 2048 + lane)
        key, major, minor = column(key_row), column(major_row), column(minor_row)
        before = key_row < key
        rank = jnp.sum(jnp.where(before, 1, 0), axis=1, keepdims=True)
        goes_on = jnp.sum(jnp.where(before & (major_row == major), 1, 0), axis=1, keepdims=True)
        hit = rank == across

        def sort(values, most):
            return jnp.minimum(jnp.sum(jnp.where(hit, values, 0), axis=0, keepdims=True), most)

        table[base:base + 1, 0:n] = sort(down, n - 1)
        table[base + 1:base + 2, 0:n] = sort(jnp.maximum(minor, 0), 31 if base else 15)
        table[base + 2:base + 3, 0:n] = sort(jnp.minimum(goes_on, 1), 1)
        upto = jnp.sum(jnp.where((major >= 0) & (major <= across), 1, 0), axis=0, keepdims=True)
        here = jnp.sum(jnp.where(major == across, 1, 0), axis=0, keepdims=True)
        table[base + 3:base + 4, 0:n] = jnp.where(here > 0, upto - 1, n)


def layer_kernel(
    features_hbm, order_hbm, weight_hbm, tiles_hbm, pairs_hbm, cotangent_hbm,
    activated, feature_grad, weight_grad,
    features, order, weight, tiles, pairs, cotangent, table, steps, load,
    blocks, prods, part, grad, back,
    from_a, from_d, from_s, staged, summed_y, from_z,
    wg, wg_core, wg_y, wg_z, wg_x, wg_zh, wg_sent, pieces,
    from_core, staged_x, from_x, own_x, zh_out, from_zh,
    row_send, row_recv,
    send_a, send_d, send_s, send_z, recv_a, recv_d, recv_s, recv_z,
    gather_send, gather_recv, wg_send, wg_recv,
    send_core, recv_core, send_x, recv_x, send_zh, recv_zh, back_send, back_recv,
):
    zh, x, k, y, zl = position()

    def on_y(d):
        return device(zh, x, k, (y + d + 4) % 4, zl)

    def on_z(z):
        return device(zh, x, k, y, z)

    def block(yy, c):
        return (yy + 4) % 4 * 8 + c

    sibling = device(zh, x, 1 - k, y, zl)
    other = device(1 - zh, x, k, y, zl)
    x_peers = [device(zh, (x + d) % 4, k, y, zl) for d in (1, 2, 3)]
    y_peers = [on_y(d) for d in (1, 2, 3)]
    z_peers = [on_z((zl + d) % 8) for d in range(1, 8)]
    everyone = [other, sibling] + x_peers + y_peers + z_peers
    barrier = pltpu.get_barrier_semaphore()
    for target in everyone:
        pl.semaphore_signal(barrier, inc=1, device_id=target, device_id_type=MESH)

    loads = [
        pltpu.make_async_copy(hbm, vmem, load.at[n])
        for n, (hbm, vmem) in enumerate((
            (features_hbm, features), (order_hbm, order), (pairs_hbm, pairs),
            (weight_hbm, weight), (cotangent_hbm, cotangent), (tiles_hbm, tiles),
        ))
    ]
    for copy in loads:
        copy.start()
    copies = []

    def go(copy):
        copy.start()
        copies.append(copy)

    def landed(buffer, sem):
        remote(buffer, buffer, sem, sem, sibling).wait_recv()

    mine = zh * 8 + x * 2 + k
    far = (1 - zh) * 8 + x * 2 + k
    loads[0].wait()
    loads[1].wait()
    blocks[mine] = dot(chosen(order[...]), features[...], ((0,), (0,))).astype(BF16)
    loads[2].wait()
    tables(pairs, table)
    to_scalars = pltpu.make_async_copy(table, steps, load.at[6])
    to_scalars.start()
    prods[96] = jnp.zeros((128, 256), BF16)
    pl.semaphore_wait(barrier, len(everyone))
    pushes = [0]

    def push(slot, target):
        go(remote(blocks.at[slot], blocks.at[slot], row_send.at[pushes[0]], row_recv.at[slot], target))
        pushes[0] += 1

    push(mine, other)
    for d in (1, 3, 2):
        push(mine, x_peers[d - 1])
    push(mine, sibling)
    for d in (1, 3, 2):
        slot = zh * 8 + (x + d) % 4 * 2 + k
        landed(blocks.at[slot], row_recv.at[slot])
        push(slot, sibling)
    landed(blocks.at[far], row_recv.at[far])
    for d in (1, 3, 2):
        push(far, x_peers[d - 1])
    push(far, sibling)
    for d in (1, 3, 2):
        slot = (1 - zh) * 8 + (x + d) % 4 * 2 + k
        landed(blocks.at[slot], row_recv.at[slot])
        push(slot, sibling)
    for copy in loads[3:]:
        copy.wait()
    to_scalars.wait()
    for n in range(8):
        slot = n * 2 + 1 - k
        landed(blocks.at[slot], row_recv.at[slot])

    def products(source, base, dims, out):
        unroll = 4

        def step(i, total):
            for j in range(unroll):
                s = i * unroll + j
                product = dot(tiles[steps[base, s]], source[steps[base + 1, s]], dims)
                total = total * steps[base + 2, s].astype(F32) + product
                prods[s] = total.astype(BF16)
            return total

        lax.fori_loop(0, 96 // unroll, step, jnp.zeros((128, 256), F32))

        def pick(b, carry):
            out[b] = prods[steps[base + 3, b]]
            return carry

        lax.fori_loop(0, out.shape[0], pick, 0)

    products(blocks, 0, ((1,), (0,)), part)

    near, half = zl % 4, zl // 4
    partner = on_z((zl + 4) % 8)
    edge = near + near // 2 * (3 - 2 * near)
    inward = 1 - 2 * (near // 2)

    def ranked(m):
        both = (2 * edge - m + 4) // 4
        alternate = 1 if m % 2 else -1
        return near + both * alternate * ((m + 1) // 2) + (1 - both) * inward * (m - edge)

    nearest = [ranked(m) for m in (1, 2, 3)]

    place = [nearest[2], nearest[1], nearest[0], near] * 2
    chunk = [(1 - half) * 4 + n for n in place[:4]] + [half * 4 + n for n in place[4:]]
    turn = [1 - 2 * (n % 2) for n in place]
    def send_antipode(i):
        c = chunk[i]
        go(remote(part.at[block(y + 2, c)], from_a.at[c], send_a.at[c], recv_a.at[c], on_y(turn[i])))

    def send_direct(i):
        c = chunk[i]
        go(remote(part.at[block(y - turn[i], c)], from_d.at[c], send_d.at[c], recv_d.at[c], on_y(-turn[i])))

    def send_sum(i):
        c = chunk[i]
        landed(from_a.at[c], recv_a.at[c])
        staged[c] = (part[block(y + turn[i], c)].astype(F32) + from_a[c].astype(F32)).astype(BF16)
        go(remote(staged.at[c], from_s.at[c], send_s.at[c], recv_s.at[c], on_y(turn[i])))

    def sum_y(i):
        c = chunk[i]
        landed(from_d.at[c], recv_d.at[c])
        landed(from_s.at[c], recv_s.at[c])
        return part[block(y, c)].astype(F32) + from_d[c].astype(F32) + from_s[c].astype(F32)

    def to_place(i):
        c = chunk[i]
        summed_y[c] = sum_y(i).astype(BF16)
        slot = i // 4 * 4 + near
        go(remote(summed_y.at[c], from_z.at[slot], send_z.at[c], recv_z.at[slot], on_z(half * 4 + place[i])))

    def sum_half(i):
        total = sum_y(i)
        for d in (1, 2, 3):
            slot = i // 4 * 4 + (near + d) % 4
            landed(from_z.at[slot], recv_z.at[slot])
            total = total + from_z[slot].astype(F32)
        return total

    send_antipode(0)
    send_antipode(1)
    send_direct(0)
    for i in range(8):
        if i + 2 < 8:
            send_antipode(i + 2)
        if i + 1 < 8:
            send_direct(i + 1)
        send_sum(i)
        if 1 <= i <= 3 or 5 <= i:
            to_place(i - 1)
        if i == 5:
            c = chunk[3]
            summed_y[c] = sum_half(3).astype(BF16)
            go(remote(summed_y.at[c], from_z.at[8], send_z.at[c], recv_z.at[8], partner))
    own = sum_half(7)
    landed(from_z.at[8], recv_z.at[8])
    own = own + from_z[8].astype(F32)

    summed = split_dot(own, weight[...], ((1,), (0,)))
    logistic = 1.0 / (1.0 + jnp.exp(-summed))
    gradient = (cotangent[...].astype(F32) * logistic * (1.0 + summed * (1.0 - logistic))).astype(BF16)
    here = block(y, zl)
    grad[here] = gradient

    def arrived(slot):
        landed(grad.at[slot], gather_recv.at[slot])

    def pass_on(slot, lane, m, target):
        go(remote(grad.at[slot], grad.at[slot], gather_send.at[lane, m], gather_recv.at[slot], target))

    def to_half(slot, lane):
        for m in range(3):
            pass_on(slot, lane, m, on_z(half * 4 + nearest[m]))

    pass_on(here, 3, 3, partner)
    to_half(here, 3)
    pass_on(here, 1, 0, on_y(1))
    pass_on(here, 2, 0, on_y(-1))
    activated[...] = (summed * logistic).astype(BF16)
    wg[...] = split_dot(own, gradient, ((0,), (0,)))
    core_copy = remote(wg.at[pl.ds((1 - k) * 128, 128)], wg_core, wg_send.at[0], wg_recv.at[0], sibling)
    go(core_copy)

    def wg_after_core():
        core_copy.wait_recv()
        wg[pl.ds(pl.multiple_of(k * 128, 128), 128)] += wg_core[...]
        for d in (1, 2, 3):
            rows = pl.ds(pl.multiple_of(k * 128 + (y + d) % 4 * 32, 32), 32)
            go(remote(wg.at[rows], wg_y.at[d], wg_send.at[d], wg_recv.at[d], y_peers[d - 1]))

    def wg_after_y():
        rows = pl.ds(pl.multiple_of(k * 128 + y * 32, 32), 32)
        total = wg[rows]
        for d in (1, 2, 3):
            landed(wg_y.at[d], wg_recv.at[d])
            total = total + wg_y[d]
        for j in range(8):
            wg_sent[j] = total[8 * (j // 2): 8 * (j // 2) + 8, 128 * (j % 2): 128 * (j % 2) + 128]
        for d in range(1, 8):
            go(remote(wg_sent.at[(zl + d) % 8], wg_z.at[d], wg_send.at[3 + d], wg_recv.at[3 + d], z_peers[d - 1]))

    def wg_after_z():
        total = wg_sent[zl]
        for d in range(1, 8):
            landed(wg_z.at[d], wg_recv.at[3 + d])
            total = total + wg_z[d]
        wg_x[x] = total
        for d in (1, 2, 3):
            go(remote(wg_x.at[x], wg_x.at[x], wg_send.at[10 + d], wg_recv.at[11 + x], x_peers[d - 1]))

    def wg_after_x():
        for d in (1, 2, 3):
            landed(wg_x.at[(x + d) % 4], wg_recv.at[11 + (x + d) % 4])
        wg_zh[zh] = wg_x[0] + wg_x[1] + wg_x[2] + wg_x[3]
        go(remote(wg_zh.at[zh], wg_zh.at[zh], wg_send.at[14], wg_recv.at[15 + zh], other))

    def wg_after_zh():
        landed(wg_zh.at[1 - zh], wg_recv.at[16 - zh])
        mine_at = pieces.at[k, y, zl]
        pieces[k, y, zl] = wg_zh[0] + wg_zh[1]
        for d in range(1, 8):
            go(remote(mine_at, mine_at, back_send.at[d], back_recv.at[zl], z_peers[d - 1]))

    def wg_back_y():
        for d in range(1, 8):
            landed(pieces.at[k, y, (zl + d) % 8], back_recv.at[(zl + d) % 8])
        for d in (1, 2, 3):
            go(remote(pieces.at[k, y], pieces.at[k, y], back_send.at[7 + d], back_recv.at[8 + y], y_peers[d - 1]))

    def wg_back_core():
        for d in (1, 2, 3):
            landed(pieces.at[k, (y + d) % 4], back_recv.at[8 + (y + d) % 4])
        go(remote(pieces.at[k], pieces.at[k], back_send.at[0], back_recv.at[12], sibling))

    def wg_finish():
        landed(pieces.at[1 - k], back_recv.at[12])
        for kk in range(2):
            for yy in range(4):
                for j in range(8):
                    row = kk * 128 + yy * 32 + j // 2 * 8
                    weight_grad[row:row + 8, j % 2 * 128:j % 2 * 128 + 128] = pieces[kk, yy, j]

    spread = [zl] + [half * 4 + n for n in nearest] + [(zl + 4) % 8] + [(1 - half) * 4 + n for n in nearest]

    def across(m):
        c = spread[m]
        e = 1 - 2 * (c % 2)
        slot = block(y - e, c)
        arrived(slot)
        pass_on(slot, 0, m, on_y(e))

    for m in range(1, 8):
        slot = block(y, spread[m])
        arrived(slot)
        if m == 4:
            to_half(slot, 4)
        pass_on(slot, 1, m, on_y(1))
        pass_on(slot, 2, m, on_y(-1))
        across(m - 1)
        if m == 2:
            wg_after_core()
        if m == 4:
            wg_after_y()
    across(7)
    wg_after_z()
    for c in range(8):
        e = 1 - 2 * (c % 2)
        arrived(block(y + e, c))
        arrived(block(y + 2, c))
    wg_after_x()

    products(grad, 4, ((0,), (0,)), back)

    for h, d in [(1 - zh, d) for d in (2, 1, 3, 0)] + [(zh, d) for d in (2, 1, 3, 0)]:
        slot = h * 4 + (x + d) % 4
        go(remote(back.at[slot * 2 + 1 - k], from_core.at[slot], send_core.at[slot], recv_core.at[slot], sibling))

    def to_x(h):
        for d in (2, 1, 3, 0):
            slot = h * 4 + (x + d) % 4
            landed(from_core.at[slot], recv_core.at[slot])
            total = back[slot * 2 + k].astype(F32) + from_core[slot].astype(F32)
            if d:
                staged_x[slot] = total.astype(BF16)
                go(remote(
                    staged_x.at[slot], from_x.at[h * 4 + d], send_x.at[slot], recv_x.at[h * 4 + d], x_peers[d - 1]
                ))
            else:
                own_x[h] = total

    def sum_x(h):
        total = own_x[h]
        for d in (1, 2, 3):
            landed(from_x.at[h * 4 + d], recv_x.at[h * 4 + d])
            total = total + from_x[h * 4 + d].astype(F32)
        return total

    to_x(1 - zh)
    wg_after_zh()
    to_x(zh)
    zh_out[...] = sum_x(1 - zh).astype(BF16)
    go(remote(zh_out, from_zh, send_zh, recv_zh, other))
    wg_back_y()
    backward = sum_x(zh)
    wg_back_core()
    wg_finish()
    landed(from_zh, recv_zh)
    backward = backward + from_zh[...].astype(F32)
    clustered_grad = split_dot(backward, weight[...], ((1,), (1,))).astype(BF16)
    feature_grad[...] = dot(chosen(order[...]), clustered_grad, ((1,), (0,))).astype(BF16)
    for copy in copies:
        copy.wait_send()


def body(features, order, weight, tile_values, tile_list, cotangent):
    dma = pltpu.SemaphoreType.DMA

    def slabs(n):
        return pltpu.VMEM((n, 128, 256), BF16)

    return pl.pallas_call(
        layer_kernel,
        out_shape=(
            jax.ShapeDtypeStruct((128, 256), BF16),
            jax.ShapeDtypeStruct((128, 256), BF16),
            jax.ShapeDtypeStruct((256, 256), F32),
        ),
        in_specs=[pl.BlockSpec(memory_space=pl.ANY)] * 6,
        out_specs=(pl.BlockSpec(memory_space=pltpu.VMEM),) * 3,
        scratch_shapes=[
            pltpu.VMEM((128, 256), BF16), pltpu.VMEM((1, 128), jnp.int32), pltpu.VMEM((256, 256), BF16),
            pltpu.VMEM((96, 128, 128), BF16), pltpu.VMEM((2, 96), jnp.int32), pltpu.VMEM((128, 256), BF16),
            pltpu.VMEM((8, 128), jnp.int32), pltpu.SMEM((8, 128), jnp.int32), dma((7,)),
            slabs(16), slabs(97), slabs(32), slabs(32), slabs(16),
            slabs(8), slabs(8), slabs(8), slabs(8), slabs(8), slabs(9),
            pltpu.VMEM((256, 256), F32), pltpu.VMEM((128, 256), F32), pltpu.VMEM((4, 32, 256), F32),
            pltpu.VMEM((8, 8, 128), F32), pltpu.VMEM((4, 8, 128), F32), pltpu.VMEM((2, 8, 128), F32),
            pltpu.VMEM((8, 8, 128), F32), pltpu.VMEM((2, 4, 8, 8, 128), F32),
            slabs(8), slabs(8), slabs(8), pltpu.VMEM((2, 128, 256), F32),
            pltpu.VMEM((128, 256), BF16), pltpu.VMEM((128, 256), BF16),
            dma((16,)), dma((16,)),
            dma((8,)), dma((8,)), dma((8,)), dma((8,)), dma((8,)), dma((8,)), dma((8,)), dma((9,)),
            dma((5, 8)), dma((32,)), dma((15,)), dma((17,)),
            dma((8,)), dma((8,)), dma((8,)), dma((8,)), dma, dma, dma((11,)), dma((13,)),
        ],
        compiler_params=pltpu.CompilerParams(collective_id=0, has_side_effects=True, vmem_limit_bytes=VMEM_LIMIT),
        name="layer",
    )(features, order, weight, tile_values[0, 0], tile_list[0, 0].T, cotangent)


def solution(mesh):
    placed = (
        P(("row", "col"), None),
        P(("row", "col"), None),
        P(),
        P("row", "col", None, None, None),
        P("row", "col", None, None),
        P(("row", "col"), None),
    )
    return jax.shard_map(
        body,
        mesh=mesh,
        in_specs=placed,
        out_specs=(P(("row", "col"), None), P(("row", "col"), None), P()),
        check_vma=False,
    )
```

time: 1220 us -> 130 us (0.11)
  waiting for transfers between devices: 1080 us -> 0 us
  Pallas kernels: 0 us -> 125 us
  other arithmetic: 63.5 us -> 0 us
  local copies, waits for them, and re-layouts: 33.6 us -> 4.61 us
  matrix products: 24.3 us -> 0 us
  between operations: 14.5 us -> 0.64 us
    psum x1 -> x0, waiting for transfers between devices: 450 us -> none  [body(): weight_grad = lax.psum(local_grad, ('row', 'col'))]
    reduce_scatter x2 -> x0, waiting for transfers between devices: 323 us -> none  [the longest x1 210 us: body(): lax.psum_scatter(partial_value.astype(jnp.bfloat16), 'col', scatter_dimen...]
    all_gather x2 -> x0, waiting for transfers between devices: 307 us -> none  [the longest x1 222 us: body(): grad_rows = lax.all_gather(summed_grad, 'col', axis=0, tiled=True)]
    pallas_call x0 -> x1, Pallas kernels: none -> 125 us  [body(): pl.pallas_call(layer_kernel, out_shape=(jax.ShapeDtypeStruct((128, 256),...]
    scatter-add x12 -> x0, other arithmetic: 53.7 us -> none  [advance(): return accumulated.at[target_block].add(products, mode='drop')]
    dot_general x17 -> x0, matrix products: 24.3 us -> none  [the longest x6 9.32 us: advance(): jnp.einsum('tij,tjf->tif', tile_piece, picked, preferred_element_type=jnp...]
    gather x12 -> x0, local copies, waits for them, and re-layouts: 24.3 us -> none  [advance(): picked = jnp.take(source_blocks, source_block, axis=0)]
  transfers between devices with their start and end apart: 5 -> 0, of which waited for: 5 -> 0; matrix products, arithmetic and copies ran while one was open for 1% -> 0% of each run, Pallas kernels for 0% -> 0%
where the time goes in v2:
time: 130 us
  Pallas kernels  125 us (96%)
  local copies, waits for them, and re-layouts  4.61 us (4%)
    pallas_call x1, Pallas kernels, body(): pl.pallas_call(layer_kernel, out_shape=(jax.ShapeDtypeStruct((128, 256),...  125 us
    unnamed x3, local copies, waits for them, and re-layouts  4.61 us

profile of v2, /device:TPU:1, one launch (start us, length us, event | category | flops | bytes accessed | tf_op | source)
XLA Modules:
  0.0 129.8 jit_solution(15259315490703309707)
XLA Ops:
  0.6 124.6 %layer.1 = (bf16[128,256]{1,0:T(8,128)(2,1)}, bf16[128,256]{1,0:T(8,128)(2,1)}, f32[256,256]{1,0:T(8,128)}) custom-call(bf16[128,256]{1,0:T(8,128)(2,1)} %features_hbm.1, s32[1,128]{1,0:T(1,128)} %order_hbm.1, bf16[256,256]{1,0:T(8,128)(2,1)} %weight_hbm.1, bf16[96,128,128]{2,1,0:T(8,128)(2,1)} %bitcast.4, s32[2,96]{1,0:T(2,128)} %bitcast.5, ...), custom_call_target="tpu_custom_call" | custom-call | tf_op jit(solution)/shard_map/layer/pallas_call | solution.py:417
  125.2 1.5 %copy.12 = bf16[128,256]{1,0:T(8,128)(2,1)} copy(bf16[128,256]{1,0:T(8,128)(2,1)} %get-tuple-element.6) | data formatting | bytes 131072
  126.7 1.5 %copy.13 = bf16[128,256]{1,0:T(8,128)(2,1)} copy(bf16[128,256]{1,0:T(8,128)(2,1)} %get-tuple-element.7) | data formatting | bytes 131072
  128.2 1.7 %copy.14 = f32[256,256]{1,0:T(8,128)} copy(f32[256,256]{1,0:T(8,128)} %get-tuple-element.8) | data formatting | bytes 524288

commit v3 on v2

v3 whole, which is shorter than its diff:
```python
import jax
import jax.numpy as jnp
from jax import lax
from jax.experimental import pallas as pl
from jax.experimental.pallas import tpu as pltpu
from jax.sharding import PartitionSpec as P

MESH = pl.DeviceIdType.MESH
F32 = jnp.float32
BF16 = jnp.bfloat16
VMEM_LIMIT = 52 << 20


def position():
    row, col = lax.axis_index("row"), lax.axis_index("col")
    return row // 8, row // 2 % 4, row % 2, col // 8, col % 8


def device(zh, x, k, y, zl):
    return {"row": zh * 8 + x * 2 + k, "col": y * 8 + zl}


def remote(src, dst, send, recv, target):
    return pltpu.make_async_remote_copy(
        src_ref=src, dst_ref=dst, send_sem=send, recv_sem=recv, device_id=target, device_id_type=MESH
    )


def dot(a, b, dims):
    return lax.dot_general(a, b, (dims, ((), ())), preferred_element_type=F32)


def split_dot(a, b, dims):
    high = a.astype(BF16)
    low = (a - high.astype(F32)).astype(BF16)
    return dot(high, b, dims) + dot(low, b, dims)


def chosen(order):
    rows = lax.broadcasted_iota(jnp.int32, (128, 128), 0)
    return jnp.where(rows == order, 1.0, 0.0).astype(BF16)


def tables(pairs, table):
    n = pairs.shape[1]
    down = lax.broadcasted_iota(jnp.int32, (n, n), 0)
    across = lax.broadcasted_iota(jnp.int32, (n, n), 1)
    same = down == across

    def column(row):
        return jnp.sum(jnp.where(same, row, 0), axis=1, keepdims=True)

    p_row, q_row = pairs[0:1, :], pairs[1:2, :]
    lane = lax.broadcasted_iota(jnp.int32, (1, n), 1)
    for base, major_row, minor_row in ((0, p_row, q_row), (4, q_row, p_row)):
        key_row = jnp.where(p_row >= 0, major_row * 32 + minor_row, 2048 + lane)
        key, major, minor = column(key_row), column(major_row), column(minor_row)
        before = key_row < key
        rank = jnp.sum(jnp.where(before, 1, 0), axis=1, keepdims=True)
        goes_on = jnp.sum(jnp.where(before & (major_row == major), 1, 0), axis=1, keepdims=True)
        hit = rank == across

        def sort(values, most):
            return jnp.minimum(jnp.sum(jnp.where(hit, values, 0), axis=0, keepdims=True), most)

        table[base:base + 1, 0:n] = sort(down, n - 1)
        table[base + 1:base + 2, 0:n] = sort(jnp.maximum(minor, 0), 31 if base else 15)
        table[base + 2:base + 3, 0:n] = sort(jnp.minimum(goes_on, 1), 1)
        upto = jnp.sum(jnp.where((major >= 0) & (major <= across), 1, 0), axis=0, keepdims=True)
        here = jnp.sum(jnp.where(major == across, 1, 0), axis=0, keepdims=True)
        table[base + 3:base + 4, 0:n] = jnp.where(here > 0, upto - 1, n)


def layer_kernel(
    features_hbm, order_hbm, weight_hbm, tiles_hbm, pairs_hbm, cotangent_hbm,
    activated, feature_grad, weight_grad,
    features, order, weight, tiles, pairs, cotangent, table, steps, load,
    blocks, prods, part, grad, back,
    from_a, from_d, from_s, staged, summed_y, from_z,
    wg, wg_core, wg_x, wg_y, wg_z,
    from_core, staged_x, from_x, own_x, zh_out, from_zh,
    row_send, row_recv,
    send_a, send_d, send_s, send_z, recv_a, recv_d, recv_s, recv_z,
    gather_send, gather_recv, wg_send, wg_recv,
    send_core, recv_core, send_x, recv_x, send_zh, recv_zh, back_send, back_recv,
):
    zh, x, k, y, zl = position()

    def on_y(d):
        return device(zh, x, k, (y + d + 4) % 4, zl)

    def on_z(z):
        return device(zh, x, k, y, z)

    def block(yy, c):
        return (yy + 4) % 4 * 8 + c

    sibling = device(zh, x, 1 - k, y, zl)
    other = device(1 - zh, x, k, y, zl)
    x_peers = [device(zh, (x + d) % 4, k, y, zl) for d in (1, 2, 3)]
    y_peers = [on_y(d) for d in (1, 2, 3)]
    z = zh * 8 + zl
    z_peers = [device((z + d) % 16 // 8, x, k, y, (z + d) % 8) for d in range(1, 16)]
    everyone = [sibling] + x_peers + y_peers + z_peers
    barrier = pltpu.get_barrier_semaphore()
    for target in everyone:
        pl.semaphore_signal(barrier, inc=1, device_id=target, device_id_type=MESH)

    loads = [
        pltpu.make_async_copy(hbm, vmem, load.at[n])
        for n, (hbm, vmem) in enumerate((
            (features_hbm, features), (order_hbm, order), (pairs_hbm, pairs),
            (weight_hbm, weight), (cotangent_hbm, cotangent), (tiles_hbm, tiles),
        ))
    ]
    for copy in loads:
        copy.start()
    copies = []

    def go(copy):
        copy.start()
        copies.append(copy)

    def landed(buffer, sem):
        remote(buffer, buffer, sem, sem, sibling).wait_recv()

    mine = zh * 8 + x * 2 + k
    far = (1 - zh) * 8 + x * 2 + k
    loads[0].wait()
    loads[1].wait()
    blocks[mine] = dot(chosen(order[...]), features[...], ((0,), (0,))).astype(BF16)
    loads[2].wait()
    tables(pairs, table)
    to_scalars = pltpu.make_async_copy(table, steps, load.at[6])
    to_scalars.start()
    prods[96] = jnp.zeros((128, 256), BF16)
    pl.semaphore_wait(barrier, len(everyone))
    pushes = [0]

    def cut_block(slot, part_of):
        return blocks.at[slot] if part_of is None else blocks.at[slot, pl.ds(part_of * 64, 64)]

    def push(slot, target, part_of=None):
        view = cut_block(slot, part_of)
        go(remote(view, view, row_send.at[pushes[0]], row_recv.at[slot, part_of or 0], target))
        pushes[0] += 1

    def got(slot, part_of=None):
        landed(cut_block(slot, part_of), row_recv.at[slot, part_of or 0])

    push(mine, other, 0)
    push(mine, other, 1)
    for d in (2, 1, 3):
        push(mine, x_peers[d - 1])
    push(mine, sibling)
    for d in (1, 3, 2):
        slot = zh * 8 + (x + d) % 4 * 2 + k
        got(slot)
        push(slot, sibling)
    for part_of in (0, 1):
        got(far, part_of)
        for d in (2, 1, 3):
            push(far, x_peers[d - 1], part_of)
        push(far, sibling, part_of)
    for part_of in (0, 1):
        for d in (1, 3, 2):
            slot = (1 - zh) * 8 + (x + d) % 4 * 2 + k
            got(slot, part_of)
            push(slot, sibling, part_of)
    for copy in loads[3:]:
        copy.wait()
    to_scalars.wait()
    for n in range(4):
        got(zh * 8 + n * 2 + 1 - k)
        got((1 - zh) * 8 + n * 2 + 1 - k, 0)
        got((1 - zh) * 8 + n * 2 + 1 - k, 1)

    def products(source, base, dims, out):
        unroll = 4

        def step(i, total):
            for j in range(unroll):
                s = i * unroll + j
                product = dot(tiles[steps[base, s]], source[steps[base + 1, s]], dims)
                total = total * steps[base + 2, s].astype(F32) + product
                prods[s] = total.astype(BF16)
            return total

        lax.fori_loop(0, 96 // unroll, step, jnp.zeros((128, 256), F32))

        def pick(b, carry):
            out[b] = prods[steps[base + 3, b]]
            return carry

        lax.fori_loop(0, out.shape[0], pick, 0)

    products(blocks, 0, ((1,), (0,)), part)

    near, half = zl % 4, zl // 4
    partner = on_z((zl + 4) % 8)
    edge = near + near // 2 * (3 - 2 * near)
    inward = 1 - 2 * (near // 2)

    def ranked(m):
        both = (2 * edge - m + 4) // 4
        alternate = 1 if m % 2 else -1
        return near + both * alternate * ((m + 1) // 2) + (1 - both) * inward * (m - edge)

    nearest = [ranked(m) for m in (1, 2, 3)]

    place = [nearest[2], nearest[1], nearest[0], near]
    units = [((1 - half) * 4 + n, n, rows, 64) for rows in (0, 64) for n in place]
    units += [(half * 4 + n, n, 0, 128) for n in place]

    def cut(buffer, index, u):
        return buffer.at[index, pl.ds(units[u][2], units[u][3])]

    def read(buffer, index, u):
        return buffer[index, pl.ds(units[u][2], units[u][3])].astype(F32)

    def sem(group, u):
        return group.at[units[u][0], units[u][2] // 64]

    def turn(u):
        return 1 - 2 * (units[u][1] % 2)

    def send_antipode(u):
        c = units[u][0]
        go(remote(cut(part, block(y + 2, c), u), cut(from_a, c, u), sem(send_a, u), sem(recv_a, u), on_y(turn(u))))

    def send_direct(u):
        c = units[u][0]
        source = cut(part, block(y - turn(u), c), u)
        go(remote(source, cut(from_d, c, u), sem(send_d, u), sem(recv_d, u), on_y(-turn(u))))

    def send_sum(u):
        c, _, rows, count = units[u]
        landed(cut(from_a, c, u), sem(recv_a, u))
        total = read(part, block(y + turn(u), c), u) + read(from_a, c, u)
        staged[c, pl.ds(rows, count)] = total.astype(BF16)
        go(remote(cut(staged, c, u), cut(from_s, c, u), sem(send_s, u), sem(recv_s, u), on_y(turn(u))))

    def sum_y(u):
        c = units[u][0]
        landed(cut(from_d, c, u), sem(recv_d, u))
        landed(cut(from_s, c, u), sem(recv_s, u))
        return read(part, block(y, c), u) + read(from_d, c, u) + read(from_s, c, u)

    def to_place(u):
        c, n, rows, count = units[u]
        summed_y[c, pl.ds(rows, count)] = sum_y(u).astype(BF16)
        slot = u // 8 * 4 + near
        arrival = recv_z.at[slot, rows // 64]
        go(remote(cut(summed_y, c, u), cut(from_z, slot, u), sem(send_z, u), arrival, on_z(half * 4 + n)))

    def sum_half(u):
        total = sum_y(u)
        for d in (1, 2, 3):
            slot = u // 8 * 4 + (near + d) % 4
            landed(cut(from_z, slot, u), recv_z.at[slot, units[u][2] // 64])
            total = total + read(from_z, slot, u)
        return total

    def to_partner(u):
        c, _, rows, count = units[u]
        summed_y[c, pl.ds(rows, count)] = sum_half(u).astype(BF16)
        arrival = recv_z.at[8, rows // 64]
        go(remote(cut(summed_y, c, u), cut(from_z, 8, u), sem(send_z, u), arrival, partner))

    def run(action, *numbers):
        for u in numbers:
            action(u)

    run(send_antipode, *range(8))
    run(send_direct, 0, 1)
    run(send_sum, 0, 1)
    run(send_direct, 2, 3)
    run(send_sum, 2, 3)
    run(send_direct, 4, 5)
    run(send_sum, 4, 5)
    run(send_direct, 6, 7)
    run(send_sum, 6, 7)
    run(send_antipode, 8, 9, 10, 11)
    run(to_place, 0, 1, 2)
    run(send_direct, 8, 9)
    run(to_place, 4, 5, 6)
    run(to_partner, 3)
    run(send_sum, 8, 9)
    run(send_direct, 10, 11)
    run(send_sum, 10, 11)
    run(to_partner, 7)
    run(to_place, 8, 9, 10)
    own = sum_half(11)
    landed(from_z.at[8, pl.ds(0, 64)], recv_z.at[8, 0])
    landed(from_z.at[8, pl.ds(64, 64)], recv_z.at[8, 1])
    own = own + from_z[8].astype(F32)

    summed = split_dot(own, weight[...], ((1,), (0,)))
    logistic = 1.0 / (1.0 + jnp.exp(-summed))
    gradient = (cotangent[...].astype(F32) * logistic * (1.0 + summed * (1.0 - logistic))).astype(BF16)
    here = block(y, zl)
    grad[here] = gradient

    def cut_grad(slot, part_of):
        return grad.at[slot] if part_of is None else grad.at[slot, pl.ds(part_of * 64, 64)]

    def arrived(slot, part_of=None):
        landed(cut_grad(slot, part_of), gather_recv.at[slot, part_of or 0])

    sent = [0]

    def pass_on(slot, part_of, target):
        view = cut_grad(slot, part_of)
        go(remote(view, view, gather_send.at[sent[0]], gather_recv.at[slot, part_of or 0], target))
        sent[0] += 1

    def to_half(slot, part_of):
        for n in nearest:
            pass_on(slot, part_of, on_z(half * 4 + n))

    def to_sides(slot, part_of=None):
        pass_on(slot, part_of, on_y(1))
        pass_on(slot, part_of, on_y(-1))

    def across(c, part_of=None):
        e = 1 - 2 * (c % 2)
        slot = block(y - e, c)
        arrived(slot, part_of)
        pass_on(slot, part_of, on_y(e))

    pass_on(here, 0, partner)
    pass_on(here, 1, partner)
    to_sides(here)
    to_half(here, None)
    activated[...] = (summed * logistic).astype(BF16)
    wg[...] = split_dot(own, gradient, ((0,), (0,)))
    core_copy = remote(wg.at[pl.ds((1 - k) * 128, 128)], wg_core, wg_send.at[0], wg_recv.at[0], sibling)
    go(core_copy)

    def wg_after_core():
        core_copy.wait_recv()
        wg[pl.ds(pl.multiple_of(k * 128, 128), 128)] += wg_core[...]
        for d in (1, 2, 3):
            rows = pl.ds(pl.multiple_of(k * 128 + (x + d) % 4 * 32, 32), 32)
            go(remote(wg.at[rows], wg_x.at[d], wg_send.at[d], wg_recv.at[d], x_peers[d - 1]))

    def wg_after_x():
        rows = pl.ds(pl.multiple_of(k * 128 + x * 32, 32), 32)
        for d in (1, 2, 3):
            landed(wg_x.at[d], wg_recv.at[d])
        wg_x[0] = wg[rows] + wg_x[1] + wg_x[2] + wg_x[3]
        for d in (1, 2, 3):
            rows = pl.ds(pl.multiple_of((y + d) % 4 * 8, 8), 8)
            go(remote(wg_x.at[0, rows], wg_y.at[d], wg_send.at[3 + d], wg_recv.at[3 + d], y_peers[d - 1]))

    def wg_after_y():
        total = wg_x[0, pl.ds(pl.multiple_of(y * 8, 8), 8)]
        for d in (1, 2, 3):
            landed(wg_y.at[d], wg_recv.at[3 + d])
            total = total + wg_y[d]
        wg_z[z] = total
        for d in range(1, 16):
            go(remote(wg_z.at[z], wg_z.at[z], wg_send.at[6 + d], wg_recv.at[7 + z], z_peers[d - 1]))

    def wg_rows(kk, xx, yy, count):
        return weight_grad.at[pl.ds(pl.multiple_of(kk * 128 + xx * 32 + yy * 8, 8), count)]

    def wg_after_z():
        for d in range(1, 16):
            landed(wg_z.at[(z + d) % 16], wg_recv.at[7 + (z + d) % 16])
        total = wg_z[0]
        for n in range(1, 16):
            total = total + wg_z[n]
        mine_at = wg_rows(k, x, y, 8)
        mine_at[...] = total
        for d in (1, 2, 3):
            go(remote(mine_at, mine_at, back_send.at[d], back_recv.at[y], y_peers[d - 1]))

    def wg_back_x():
        for d in (1, 2, 3):
            landed(wg_rows(k, x, (y + d) % 4, 8), back_recv.at[(y + d) % 4])
        mine_at = wg_rows(k, x, 0, 32)
        for d in (1, 2, 3):
            go(remote(mine_at, mine_at, back_send.at[3 + d], back_recv.at[4 + x], x_peers[d - 1]))

    def wg_back_core():
        for d in (1, 2, 3):
            landed(wg_rows(k, (x + d) % 4, 0, 32), back_recv.at[4 + (x + d) % 4])
        mine_at = wg_rows(k, 0, 0, 128)
        go(remote(mine_at, mine_at, back_send.at[0], back_recv.at[8], sibling))

    def wg_finish():
        landed(wg_rows(1 - k, 0, 0, 128), back_recv.at[8])

    close = [half * 4 + n for n in nearest]
    beyond = (zl + 4) % 8
    distant = [(1 - half) * 4 + n for n in nearest]

    def take(c, part_of=None):
        slot = block(y, c)
        arrived(slot, part_of)
        if c is beyond:
            to_half(slot, part_of)
        to_sides(slot, part_of)

    for c in close:
        take(c)
    across(zl)
    wg_after_core()
    take(beyond, 0)
    across(close[0])
    take(beyond, 1)
    across(close[1])
    across(close[2])
    wg_after_x()
    for c in distant:
        take(c, 0)
    across(beyond, 0)
    for c in distant:
        take(c, 1)
    across(beyond, 1)
    for c in distant:
        across(c, 0)
    wg_after_y()
    for c in distant:
        across(c, 1)
    for c in [zl] + close:
        e = 1 - 2 * (c % 2)
        arrived(block(y + e, c))
        arrived(block(y + 2, c))
    for c in [beyond] + distant:
        e = 1 - 2 * (c % 2)
        for part_of in (0, 1):
            arrived(block(y + e, c), part_of)
            arrived(block(y + 2, c), part_of)
    products(grad, 4, ((0,), (0,)), back)

    for h, d in [(1 - zh, d) for d in (2, 1, 3, 0)] + [(zh, d) for d in (2, 1, 3, 0)]:
        slot = h * 4 + (x + d) % 4
        go(remote(back.at[slot * 2 + 1 - k], from_core.at[slot], send_core.at[slot], recv_core.at[slot], sibling))

    def exchanged(h):
        for d in (2, 1, 3, 0):
            slot = h * 4 + (x + d) % 4
            landed(from_core.at[slot], recv_core.at[slot])

    def to_x(h, rows, count):
        some = pl.ds(rows, count)
        for d in (2, 1, 3, 0):
            slot = h * 4 + (x + d) % 4
            total = back[slot * 2 + k, some].astype(F32) + from_core[slot, some].astype(F32)
            if d:
                staged_x[slot, some] = total.astype(BF16)
                go(remote(
                    staged_x.at[slot, some], from_x.at[h * 4 + d, some], send_x.at[slot, rows // 64],
                    recv_x.at[h * 4 + d, rows // 64], x_peers[d - 1]
                ))
            else:
                own_x[h, some] = total

    def sum_x(h, rows, count):
        some = pl.ds(rows, count)
        total = own_x[h, some]
        for d in (1, 3, 2):
            landed(from_x.at[h * 4 + d, some], recv_x.at[h * 4 + d, rows // 64])
            total = total + from_x[h * 4 + d, some].astype(F32)
        return total

    wg_after_z()
    exchanged(1 - zh)
    to_x(1 - zh, 0, 64)
    to_x(1 - zh, 64, 64)
    exchanged(zh)
    to_x(zh, 0, 128)
    for n in (0, 1):
        some = pl.ds(n * 64, 64)
        zh_out[some] = sum_x(1 - zh, n * 64, 64).astype(BF16)
        go(remote(zh_out.at[some], from_zh.at[some], send_zh.at[n], recv_zh.at[n], other))
    wg_back_x()
    backward = sum_x(zh, 0, 128)
    wg_back_core()
    wg_finish()
    for n in (0, 1):
        landed(from_zh.at[pl.ds(n * 64, 64)], recv_zh.at[n])
    backward = backward + from_zh[...].astype(F32)
    clustered_grad = split_dot(backward, weight[...], ((1,), (1,))).astype(BF16)
    feature_grad[...] = dot(chosen(order[...]), clustered_grad, ((1,), (0,))).astype(BF16)
    for copy in copies:
        copy.wait_send()


def body(features, order, weight, tile_values, tile_list, cotangent):
    dma = pltpu.SemaphoreType.DMA

    def slabs(n):
        return pltpu.VMEM((n, 128, 256), BF16)

    return pl.pallas_call(
        layer_kernel,
        out_shape=(
            jax.ShapeDtypeStruct((128, 256), BF16),
            jax.ShapeDtypeStruct((128, 256), BF16),
            jax.ShapeDtypeStruct((256, 256), F32),
        ),
        in_specs=[pl.BlockSpec(memory_space=pltpu.HBM)] * 6,
        out_specs=(pl.BlockSpec(memory_space=pltpu.VMEM),) * 3,
        scratch_shapes=[
            pltpu.VMEM((128, 256), BF16), pltpu.VMEM((1, 128), jnp.int32), pltpu.VMEM((256, 256), BF16),
            pltpu.VMEM((96, 128, 128), BF16), pltpu.VMEM((2, 96), jnp.int32), pltpu.VMEM((128, 256), BF16),
            pltpu.VMEM((8, 128), jnp.int32), pltpu.SMEM((8, 128), jnp.int32), dma((7,)),
            slabs(16), slabs(97), slabs(32), slabs(32), slabs(16),
            slabs(8), slabs(8), slabs(8), slabs(8), slabs(8), slabs(9),
            pltpu.VMEM((256, 256), F32), pltpu.VMEM((128, 256), F32), pltpu.VMEM((4, 32, 256), F32),
            pltpu.VMEM((4, 8, 256), F32), pltpu.VMEM((16, 8, 256), F32),
            slabs(8), slabs(8), slabs(8), pltpu.VMEM((2, 128, 256), F32),
            pltpu.VMEM((128, 256), BF16), pltpu.VMEM((128, 256), BF16),
            dma((23,)), dma((16, 2)),
            dma((8, 2)), dma((8, 2)), dma((8, 2)), dma((8, 2)), dma((8, 2)), dma((8, 2)), dma((8, 2)), dma((9, 2)),
            dma((53,)), dma((32, 2)), dma((22,)), dma((23,)),
            dma((8,)), dma((8,)), dma((8, 2)), dma((8, 2)), dma((2,)), dma((2,)), dma((7,)), dma((9,)),
        ],
        compiler_params=pltpu.CompilerParams(collective_id=0, has_side_effects=True, vmem_limit_bytes=VMEM_LIMIT),
        name="layer",
    )(features, order, weight, tile_values[0, 0], tile_list[0, 0].T, cotangent)


def solution(mesh):
    placed = (
        P(("row", "col"), None),
        P(("row", "col"), None),
        P(),
        P("row", "col", None, None, None),
        P("row", "col", None, None),
        P(("row", "col"), None),
    )
    return jax.shard_map(
        body,
        mesh=mesh,
        in_specs=placed,
        out_specs=(P(("row", "col"), None), P(("row", "col"), None), P()),
        check_vma=False,
    )
```

time: 130 us -> 123 us (0.946)
  Pallas kernels: 125 us -> 116 us
    pallas_call x1, Pallas kernels: 125 us -> 116 us  [body(): pl.pallas_call(layer_kernel, out_shape=(jax.ShapeDtypeStruct((128, 256),...]
    unnamed x3 -> x13, local copies, waits for them, and re-layouts: 4.61 us -> 5.87 us
where the time goes in v3:
time: 123 us; the launch traced here: 122 us
  Pallas kernels  116 us (94%)
  local copies, waits for them, and re-layouts  5.87 us (5%)
    pallas_call x1, Pallas kernels, body(): pl.pallas_call(layer_kernel, out_shape=(jax.ShapeDtypeStruct((128, 256),...  116 us
    unnamed x13, local copies, waits for them, and re-layouts  5.87 us

profile of v3, /device:TPU:1, one launch (start us, length us, event | category | flops | bytes accessed | tf_op | source)
XLA Modules:
  0.0 122.3 jit_solution(13443202958055557904)
XLA Ops:
  0.6 0.0 copy-start
  0.6 0.9 copy-done
  1.5 0.0 copy-start.1
  1.5 0.8 copy-done.1
  2.4 0.0 copy-start.2
  2.4 0.8 copy-done.2
  3.2 0.0 copy-start.3
  3.2 0.7 copy-done.3
  3.9 0.0 copy-start.4
  3.9 0.7 copy-done.4
  4.6 115.8 %layer.1 = (bf16[128,256]{1,0:T(8,128)(2,1)S(1)}, bf16[128,256]{1,0:T(8,128)(2,1)S(1)}, f32[256,256]{1,0:T(8,128)S(1)}) custom-call(bf16[128,256]{1,0:T(8,128)(2,1)S(1)} %copy-done.1, s32[1,128]{1,0:T(1,128)S(1)} %copy-done.4, bf16[256,256]{1,0:T(8,128)(2,1)S(1)} %copy-done, bf16[96,128,128]{2,1,0:T(8,128)(2,1)} %bitcast.5, s32[2,96]{1,0:T(2,128)S(1)} %bitcast.4, ...), custom_call_target="tpu_custom_call" | custom-call | tf_op jit(solution)/shard_map/layer/pallas_call | solution.py:498
  120.3 0.6 copy.12
  121.0 0.6 copy.13
  121.6 0.7 copy.14
Async XLA Ops:
  0.6 0.9 copy-start
  1.5 0.8 copy-start.1
  2.4 0.8 copy-start.2
  3.2 0.7 copy-start.3
  3.9 0.7 copy-start.4

commit v4 on v3

--- a/solution.py
+++ b/solution.py
@@ -175,8 +175,8 @@
         got((1 - zh) * 8 + n * 2 + 1 - k, 0)
         got((1 - zh) * 8 + n * 2 + 1 - k, 1)
 
-    def products(source, base, dims, out):
-        unroll = 4
+    def products(source, base, dims):
+        unroll = 32
 
         def step(i, total):
             for j in range(unroll):
@@ -188,13 +188,10 @@
 
         lax.fori_loop(0, 96 // unroll, step, jnp.zeros((128, 256), F32))
 
-        def pick(b, carry):
-            out[b] = prods[steps[base + 3, b]]
-            return carry
-
-        lax.fori_loop(0, out.shape[0], pick, 0)
-
-    products(blocks, 0, ((1,), (0,)), part)
+    def pick(out, b, base):
+        out[b] = prods[steps[base + 3, b]]
+
+    products(blocks, 0, ((1,), (0,)))
 
     near, half = zl % 4, zl // 4
     partner = on_z((zl + 4) % 8)
@@ -271,16 +268,27 @@
         for u in numbers:
             action(u)
 
-    run(send_antipode, *range(8))
-    run(send_direct, 0, 1)
+    for i in range(4):
+        pick(part, block(y + 2, units[i][0]), 0)
+        send_antipode(i)
+    run(send_antipode, 4, 5, 6, 7)
+    for i in range(4):
+        pick(part, block(y - turn(i), units[i][0]), 0)
+        send_direct(i)
+    for i in range(4):
+        pick(part, block(y + turn(i), units[i][0]), 0)
+        pick(part, block(y, units[i][0]), 0)
     run(send_sum, 0, 1)
-    run(send_direct, 2, 3)
+    run(send_direct, 4, 5)
     run(send_sum, 2, 3)
-    run(send_direct, 4, 5)
-    run(send_sum, 4, 5)
     run(send_direct, 6, 7)
-    run(send_sum, 6, 7)
-    run(send_antipode, 8, 9, 10, 11)
+    run(send_sum, 4, 5, 6, 7)
+    for i in range(8, 12):
+        pick(part, block(y + 2, units[i][0]), 0)
+        send_antipode(i)
+    for i in range(8, 12):
+        for d in (1, 3, 0):
+            pick(part, block(y + d, units[i][0]), 0)
     run(to_place, 0, 1, 2)
     run(send_direct, 8, 9)
     run(to_place, 4, 5, 6)
@@ -433,11 +441,15 @@
         for part_of in (0, 1):
             arrived(block(y + e, c), part_of)
             arrived(block(y + 2, c), part_of)
-    products(grad, 4, ((0,), (0,)), back)
-
-    for h, d in [(1 - zh, d) for d in (2, 1, 3, 0)] + [(zh, d) for d in (2, 1, 3, 0)]:
+    products(grad, 4, ((0,), (0,)))
+
+    turns = [(h, d) for h in (1 - zh, zh) for d in (2, 1, 3, 0)]
+    for h, d in turns:
         slot = h * 4 + (x + d) % 4
+        pick(back, slot * 2 + 1 - k, 4)
         go(remote(back.at[slot * 2 + 1 - k], from_core.at[slot], send_core.at[slot], recv_core.at[slot], sibling))
+    for h, d in turns:
+        pick(back, (h * 4 + (x + d) % 4) * 2 + k, 4)
 
     def exchanged(h):
         for d in (2, 1, 3, 0):
@@ -466,12 +478,12 @@
             total = total + from_x[h * 4 + d, some].astype(F32)
         return total
 
-    wg_after_z()
     exchanged(1 - zh)
     to_x(1 - zh, 0, 64)
     to_x(1 - zh, 64, 64)
     exchanged(zh)
     to_x(zh, 0, 128)
+    wg_after_z()
     for n in (0, 1):
         some = pl.ds(n * 64, 64)
         zh_out[some] = sum_x(1 - zh, n * 64, 64).astype(BF16)
@@ -479,14 +491,17 @@
     wg_back_x()
     backward = sum_x(zh, 0, 128)
     wg_back_core()
+    for copy in copies:
+        copy.wait_send()
     wg_finish()
+    placed = chosen(order[...])
+    total = jnp.zeros((128, 256), F32)
     for n in (0, 1):
         landed(from_zh.at[pl.ds(n * 64, 64)], recv_zh.at[n])
-    backward = backward + from_zh[...].astype(F32)
-    clustered_grad = split_dot(backward, weight[...], ((1,), (1,))).astype(BF16)
-    feature_grad[...] = dot(chosen(order[...]), clustered_grad, ((1,), (0,))).astype(BF16)
-    for copy in copies:
-        copy.wait_send()
+        rows = backward[n * 64:n * 64 + 64] + from_zh[n * 64:n * 64 + 64].astype(F32)
+        clustered_grad = split_dot(rows, weight[...], ((1,), (1,))).astype(BF16)
+        total = total + dot(placed[:, n * 64:n * 64 + 64], clustered_grad, ((1,), (0,)))
+    feature_grad[...] = total.astype(BF16)
 
 
 def body(features, order, weight, tile_values, tile_list, cotangent):
@@ -495,6 +510,7 @@
     def slabs(n):
         return pltpu.VMEM((n, 128, 256), BF16)
 
+    operands = (features, order, weight, tile_values[0, 0], tile_list[0, 0].T, cotangent)
     return pl.pallas_call(
         layer_kernel,
         out_shape=(
@@ -521,7 +537,7 @@
         ],
         compiler_params=pltpu.CompilerParams(collective_id=0, has_side_effects=True, vmem_limit_bytes=VMEM_LIMIT),
         name="layer",
-    )(features, order, weight, tile_values[0, 0], tile_list[0, 0].T, cotangent)
+    )(*[pltpu.with_memory_space_constraint(operand, pltpu.HBM) for operand in operands])
 
 
 def solution(mesh):

time: 123 us -> 112 us (0.911)
  Pallas kernels: 116 us -> 109 us
  local copies, waits for them, and re-layouts: 5.87 us -> 1.96 us
    pallas_call x1, Pallas kernels: 116 us -> 109 us  [body(): pl.pallas_call(layer_kernel, out_shape=(jax.ShapeDtypeStruct((128, 256),...]
    unnamed x13 -> x3, local copies, waits for them, and re-layouts: 5.87 us -> 1.96 us
where the time goes in v4:
time: 112 us; the launch traced here: 111 us
  Pallas kernels  109 us (97%)
  local copies, waits for them, and re-layouts  1.96 us (2%)
    pallas_call x1, Pallas kernels, body(): pl.pallas_call(layer_kernel, out_shape=(jax.ShapeDtypeStruct((128, 256),...  109 us

profile of v4, /device:TPU:1, one launch (start us, length us, event | category | flops | bytes accessed | tf_op | source)
XLA Modules:
  0.0 111.5 jit_solution(8905263558442313206)
XLA Ops:
  0.6 108.9 %layer.1 = (bf16[128,256]{1,0:T(8,128)(2,1)S(1)}, bf16[128,256]{1,0:T(8,128)(2,1)S(1)}, f32[256,256]{1,0:T(8,128)S(1)}) custom-call(bf16[128,256]{1,0:T(8,128)(2,1)} %features_hbm.1, s32[1,128]{1,0:T(1,128)} %order_hbm.1, bf16[256,256]{1,0:T(8,128)(2,1)} %weight_hbm.1, bf16[96,128,128]{2,1,0:T(8,128)(2,1)} %bitcast.4, s32[2,96]{1,0:T(2,128)} %bitcast.5, ...), custom_call_target="tpu_custom_call" | custom-call | tf_op jit(solution)/shard_map/layer/pallas_call | solution.py:514
  109.5 0.6 copy.12
  110.1 0.6 copy.13
  110.8 0.7 copy.14

commit v5 on v4

--- a/solution.py
+++ b/solution.py
@@ -130,10 +130,6 @@
     loads[1].wait()
     blocks[mine] = dot(chosen(order[...]), features[...], ((0,), (0,))).astype(BF16)
     loads[2].wait()
-    tables(pairs, table)
-    to_scalars = pltpu.make_async_copy(table, steps, load.at[6])
-    to_scalars.start()
-    prods[96] = jnp.zeros((128, 256), BF16)
     pl.semaphore_wait(barrier, len(everyone))
     pushes = [0]
 
@@ -153,6 +149,10 @@
     for d in (2, 1, 3):
         push(mine, x_peers[d - 1])
     push(mine, sibling)
+    tables(pairs, table)
+    to_scalars = pltpu.make_async_copy(table, steps, load.at[6])
+    to_scalars.start()
+    prods[96] = jnp.zeros((128, 256), BF16)
     for d in (1, 3, 2):
         slot = zh * 8 + (x + d) % 4 * 2 + k
         got(slot)
@@ -207,7 +207,7 @@
 
     place = [nearest[2], nearest[1], nearest[0], near]
     units = [((1 - half) * 4 + n, n, rows, 64) for rows in (0, 64) for n in place]
-    units += [(half * 4 + n, n, 0, 128) for n in place]
+    units += [(half * 4 + n, n, rows, 64) for rows in (0, 64) for n in place]
 
     def cut(buffer, index, u):
         return buffer.at[index, pl.ds(units[u][2], units[u][3])]
@@ -278,36 +278,43 @@
     for i in range(4):
         pick(part, block(y + turn(i), units[i][0]), 0)
         pick(part, block(y, units[i][0]), 0)
-    run(send_sum, 0, 1)
-    run(send_direct, 4, 5)
-    run(send_sum, 2, 3)
-    run(send_direct, 6, 7)
-    run(send_sum, 4, 5, 6, 7)
+    run(send_sum, 0, 1, 2, 3)
     for i in range(8, 12):
         pick(part, block(y + 2, units[i][0]), 0)
         send_antipode(i)
+    run(send_direct, 4, 5, 6, 7)
+    run(send_sum, 4, 5, 6, 7)
+    run(send_antipode, 12, 13, 14, 15)
     for i in range(8, 12):
         for d in (1, 3, 0):
             pick(part, block(y + d, units[i][0]), 0)
+    run(send_direct, 8, 9, 10, 11)
     run(to_place, 0, 1, 2)
-    run(send_direct, 8, 9)
+    run(send_sum, 8, 9, 10, 11)
+    run(send_direct, 12, 13, 14, 15)
     run(to_place, 4, 5, 6)
+    run(send_sum, 12, 13, 14, 15)
     run(to_partner, 3)
-    run(send_sum, 8, 9)
-    run(send_direct, 10, 11)
-    run(send_sum, 10, 11)
+    run(to_place, 8, 9, 10)
     run(to_partner, 7)
-    run(to_place, 8, 9, 10)
-    own = sum_half(11)
-    landed(from_z.at[8, pl.ds(0, 64)], recv_z.at[8, 0])
-    landed(from_z.at[8, pl.ds(64, 64)], recv_z.at[8, 1])
-    own = own + from_z[8].astype(F32)
-
-    summed = split_dot(own, weight[...], ((1,), (0,)))
-    logistic = 1.0 / (1.0 + jnp.exp(-summed))
-    gradient = (cotangent[...].astype(F32) * logistic * (1.0 + summed * (1.0 - logistic))).astype(BF16)
+    run(to_place, 12, 13, 14)
+
     here = block(y, zl)
-    grad[here] = gradient
+
+    def activate(n):
+        some = pl.ds(n * 64, 64)
+        own = sum_half(11 + 4 * n)
+        landed(from_z.at[8, some], recv_z.at[8, n])
+        own = own + from_z[8, some].astype(F32)
+        summed = split_dot(own, weight[...], ((1,), (0,)))
+        logistic = 1.0 / (1.0 + jnp.exp(-summed))
+        slope = (cotangent[some].astype(F32) * logistic * (1.0 + summed * (1.0 - logistic))).astype(BF16)
+        grad[here, some] = slope
+        pass_on(here, n, partner)
+        to_half(here, n)
+        to_sides(here, n)
+        activated[some] = (summed * logistic).astype(BF16)
+        return split_dot(own, slope, ((0,), (0,)))
 
     def cut_grad(slot, part_of):
         return grad.at[slot] if part_of is None else grad.at[slot, pl.ds(part_of * 64, 64)]
@@ -336,14 +343,7 @@
         arrived(slot, part_of)
         pass_on(slot, part_of, on_y(e))
 
-    pass_on(here, 0, partner)
-    pass_on(here, 1, partner)
-    to_sides(here)
-    to_half(here, None)
-    activated[...] = (summed * logistic).astype(BF16)
-    wg[...] = split_dot(own, gradient, ((0,), (0,)))
     core_copy = remote(wg.at[pl.ds((1 - k) * 128, 128)], wg_core, wg_send.at[0], wg_recv.at[0], sibling)
-    go(core_copy)
 
     def wg_after_core():
         core_copy.wait_recv()
@@ -411,36 +411,40 @@
             to_half(slot, part_of)
         to_sides(slot, part_of)
 
+    wg_top = activate(0)
     for c in close:
-        take(c)
-    across(zl)
+        take(c, 0)
+    across(zl, 0)
+    wg[...] = wg_top + activate(1)
+    go(core_copy)
+    take(beyond, 0)
+    for c in close:
+        across(c, 0)
+    for c in close:
+        take(c, 1)
+    across(zl, 1)
     wg_after_core()
-    take(beyond, 0)
-    across(close[0])
+    for c in distant:
+        take(c, 0)
     take(beyond, 1)
-    across(close[1])
-    across(close[2])
+    across(beyond, 0)
+    for c in close:
+        across(c, 1)
     wg_after_x()
     for c in distant:
-        take(c, 0)
-    across(beyond, 0)
+        across(c, 0)
     for c in distant:
         take(c, 1)
     across(beyond, 1)
-    for c in distant:
-        across(c, 0)
     wg_after_y()
     for c in distant:
         across(c, 1)
-    for c in [zl] + close:
-        e = 1 - 2 * (c % 2)
-        arrived(block(y + e, c))
-        arrived(block(y + 2, c))
-    for c in [beyond] + distant:
-        e = 1 - 2 * (c % 2)
-        for part_of in (0, 1):
+    for part_of in (0, 1):
+        for c in range(8):
+            e = 1 - 2 * (c % 2)
             arrived(block(y + e, c), part_of)
             arrived(block(y + 2, c), part_of)
+
     products(grad, 4, ((0,), (0,)))
 
     turns = [(h, d) for h in (1 - zh, zh) for d in (2, 1, 3, 0)]
@@ -532,7 +536,7 @@
             pltpu.VMEM((128, 256), BF16), pltpu.VMEM((128, 256), BF16),
             dma((23,)), dma((16, 2)),
             dma((8, 2)), dma((8, 2)), dma((8, 2)), dma((8, 2)), dma((8, 2)), dma((8, 2)), dma((8, 2)), dma((9, 2)),
-            dma((53,)), dma((32, 2)), dma((22,)), dma((23,)),
+            dma((62,)), dma((32, 2)), dma((22,)), dma((23,)),
             dma((8,)), dma((8,)), dma((8, 2)), dma((8, 2)), dma((2,)), dma((2,)), dma((7,)), dma((9,)),
         ],
         compiler_params=pltpu.CompilerParams(collective_id=0, has_side_effects=True, vmem_limit_bytes=VMEM_LIMIT),

time: 112 us -> 110 us (0.982)
    pallas_call x1, Pallas kernels: 109 us -> 108 us  [body(): pl.pallas_call(layer_kernel, out_shape=(jax.ShapeDtypeStruct((128, 256),...]
where the time goes in v5:
time: 110 us
  Pallas kernels  108 us (98%)
  local copies, waits for them, and re-layouts  1.96 us (2%)
    pallas_call x1, Pallas kernels, body(): pl.pallas_call(layer_kernel, out_shape=(jax.ShapeDtypeStruct((128, 256),...  108 us

profile of v5, /device:TPU:1, one launch (start us, length us, event | category | flops | bytes accessed | tf_op | source)
XLA Modules:
  0.0 110.2 jit_solution(11588850060304391005)
XLA Ops:
  0.6 107.6 %layer.1 = (bf16[128,256]{1,0:T(8,128)(2,1)S(1)}, bf16[128,256]{1,0:T(8,128)(2,1)S(1)}, f32[256,256]{1,0:T(8,128)S(1)}) custom-call(bf16[128,256]{1,0:T(8,128)(2,1)} %features_hbm.1, s32[1,128]{1,0:T(1,128)} %order_hbm.1, bf16[256,256]{1,0:T(8,128)(2,1)} %weight_hbm.1, bf16[96,128,128]{2,1,0:T(8,128)(2,1)} %bitcast.4, s32[2,96]{1,0:T(2,128)} %bitcast.5, ...), custom_call_target="tpu_custom_call" | custom-call | tf_op jit(solution)/shard_map/layer/pallas_call | solution.py:518
  108.2 0.6 copy.12
  108.9 0.6 copy.13
  109.5 0.7 copy.14

commit v6 on v5

--- a/solution.py
+++ b/solution.py
@@ -101,7 +101,7 @@
     y_peers = [on_y(d) for d in (1, 2, 3)]
     z = zh * 8 + zl
     z_peers = [device((z + d) % 16 // 8, x, k, y, (z + d) % 8) for d in range(1, 16)]
-    everyone = [sibling] + x_peers + y_peers + z_peers
+    everyone = [z_peers[8 + d - 1] for d in (0, -1, 1, -2, 2, -3, 3, -4, 4, -5, 5, -6, 6, -7, 7)] + x_peers + y_peers + [sibling]
     barrier = pltpu.get_barrier_semaphore()
     for target in everyone:
         pl.semaphore_signal(barrier, inc=1, device_id=target, device_id_type=MESH)

time: 110 us -> 109 us (level)
  no operation moved by 1% of the time
where the time goes in v6:
time: 109 us
  Pallas kernels  107 us (98%)
  local copies, waits for them, and re-layouts  1.96 us (2%)
    pallas_call x1, Pallas kernels, body(): pl.pallas_call(layer_kernel, out_shape=(jax.ShapeDtypeStruct((128, 256),...  107 us

profile of v6, /device:TPU:1, one launch (start us, length us, event | category | flops | bytes accessed | tf_op | source)
XLA Modules:
  0.0 109.4 jit_solution(6320592087110518217)
XLA Ops:
  0.6 106.8 %layer.1 = (bf16[128,256]{1,0:T(8,128)(2,1)S(1)}, bf16[128,256]{1,0:T(8,128)(2,1)S(1)}, f32[256,256]{1,0:T(8,128)S(1)}) custom-call(bf16[128,256]{1,0:T(8,128)(2,1)} %features_hbm.1, s32[1,128]{1,0:T(1,128)} %order_hbm.1, bf16[256,256]{1,0:T(8,128)(2,1)} %weight_hbm.1, bf16[96,128,128]{2,1,0:T(8,128)(2,1)} %bitcast.4, s32[2,96]{1,0:T(2,128)} %bitcast.5, ...), custom_call_target="tpu_custom_call" | custom-call | tf_op jit(solution)/shard_map/layer/pallas_call | solution.py:518
  107.4 0.6 copy.12
  108.0 0.6 copy.13
  108.7 0.7 copy.14
